TPU v7x, 32 devices: a whole 2x2x4 slice. The times are simulated.
32 devices in a mesh: groups: 1, fsdp: 32 (over z, y, x, core).
Axes of the slice: x: 2, y: 2, z: 4, core: 2. Of those that a mesh axis runs over, the one named last changes fastest.
Arguments:
- tokens: bfloat16 [6144, 8192], P(('groups', 'fsdp')), may hold values from -6 to 6
- out_grad: bfloat16 [6144, 512], P(('groups', 'fsdp')), may hold values from -12 to 12
- base_weight: bfloat16 [8192, 512], P('fsdp'), may hold values from -0.0625 to 0.0625
- adapter_ids: int32 [6144], P(('groups', 'fsdp')), may hold values from 0 to 31, as said below
- adapter_home: int32 [32], P('groups'), may hold values from 0 to 31, each once
- factors: float32 [32, 16, 8704], P(('groups', 'fsdp')), may hold values from -6 to 6
- first_moment: float32 [32, 16, 8704], P(('groups', 'fsdp'))
- second_moment: float32 [32, 16, 8704], P(('groups', 'fsdp'))
Outputs:
- value_output: bfloat16 [6144, 512], P(('groups', 'fsdp'))
- input_gradient: bfloat16 [6144, 8192], P(('groups', 'fsdp'))
- new_factors: float32 [32, 16, 8704], P(('groups', 'fsdp'))
- new_first: float32 [32, 16, 8704], P(('groups', 'fsdp'))
- new_second: float32 [32, 16, 8704], P(('groups', 'fsdp'))
Inputs may be any that keep to these rules, and one draw needn't show every extreme that they name: `adapter_ids`: on each device every adapter has between 0 and 12 tokens; one adapter, the same on all devices, has exactly 12 tokens on every device; on each device the adapters fall into pairs whose counts sum to 12. Adapter k's factors and moments are held on the device whose fsdp index is adapter_home[k]; every index appears once.
All inputs are finite; a program needn't handle non-finite values.
Results may differ from a plain program's by a relative error of at most 0.0062.
Values may be sent and summed in bfloat16 or wider, within the bound.
No kernel may reach another device: no remote copies, remote signals or barrier semaphores. Data moves between devices by JAX's collectives and lax.ppermute only.
A program may use at most 128 MiB of HBM per device.

v0:
```python
import math

import jax
import jax.numpy as jnp
from jax import lax
from jax.sharding import PartitionSpec as P

adapter_scale = 0.25
beta_first = 0.9
beta_second = 0.95
adam_eps = 1e-08
learn_rate = 0.05
bias_first = 0.271
bias_second = 0.142625
contract_last = (((1,), (1,)), ((), ()))
contract_first = (((0,), (0,)), ((), ()))


def adapter_forward_pass(
    slot_token_rows, down_projection_matrix, up_projection_matrix, input_scale
):
    projected_rows = (
        input_scale
        * lax.dot_general(
            slot_token_rows,
            down_projection_matrix,
            contract_last,
            preferred_element_type=jnp.float32,
        )
    ).astype(jnp.bfloat16)
    adapter_value = (
        adapter_scale
        * jnp.dot(projected_rows, up_projection_matrix, preferred_element_type=jnp.float32)
    ).astype(jnp.bfloat16)
    return (projected_rows, adapter_value)


def adapter_backward_pass(
    slot_token_rows,
    slot_gradient_rows,
    projected_rows,
    down_projection_matrix,
    up_projection_matrix,
    input_scale,
):
    narrow_gradient = (
        adapter_scale
        * lax.dot_general(
            slot_gradient_rows,
            up_projection_matrix,
            contract_last,
            preferred_element_type=jnp.float32,
        )
    ).astype(jnp.bfloat16)
    adapter_input = (
        input_scale
        * jnp.dot(narrow_gradient, down_projection_matrix, preferred_element_type=jnp.float32)
    ).astype(jnp.bfloat16)
    down_weight_gradient = input_scale * lax.dot_general(
        narrow_gradient, slot_token_rows, contract_first, preferred_element_type=jnp.float32
    )
    up_weight_gradient = adapter_scale * lax.dot_general(
        projected_rows, slot_gradient_rows, contract_first, preferred_element_type=jnp.float32
    )
    return (adapter_input, jnp.concatenate([down_weight_gradient, up_weight_gradient], axis=1))


def local(
    tokens, out_grad, base_weight, adapter_ids, adapter_home, factors, first_moment, second_moment
):
    tok_count, feature_width = tokens.shape
    value_width = out_grad.shape[1]
    devices = lax.axis_size("fsdp")
    capacity = 2 * tok_count // devices
    input_scale = 1.0 / math.sqrt(feature_width)
    columns = jnp.arange(devices, dtype=jnp.int32)
    adapter_hot = (adapter_ids[:, None] == columns[None, :]).astype(jnp.int32)
    target = jnp.sum(adapter_hot * adapter_home[None, :], axis=1)
    target_hot = (target[:, None] == columns[None, :]).astype(jnp.int32)
    position = jnp.sum(target_hot * (jnp.cumsum(target_hot, axis=0) - 1), axis=1)
    slot_index = target * capacity + position
    send_tokens = (
        jnp.zeros((devices * capacity, feature_width), jnp.bfloat16).at[slot_index].set(tokens)
    )
    send_grads = (
        jnp.zeros((devices * capacity, value_width), jnp.bfloat16).at[slot_index].set(out_grad)
    )
    slot_token_rows, slot_gradient_rows = (
        lax.all_to_all(send_tokens, "fsdp", split_axis=0, concat_axis=0, tiled=True),
        lax.all_to_all(send_grads, "fsdp", split_axis=0, concat_axis=0, tiled=True),
    )
    compute = factors[0].astype(jnp.bfloat16)
    down_projection_matrix = compute[:, :feature_width]
    up_projection_matrix = compute[:, feature_width:]
    projected_rows, adapter_value = adapter_forward_pass(
        slot_token_rows, down_projection_matrix, up_projection_matrix, input_scale
    )
    adapter_input, gradient_list = adapter_backward_pass(
        slot_token_rows,
        slot_gradient_rows,
        projected_rows,
        down_projection_matrix,
        up_projection_matrix,
        input_scale,
    )
    home_values, home_inputs = (
        lax.all_to_all(adapter_value, "fsdp", split_axis=0, concat_axis=0, tiled=True),
        lax.all_to_all(adapter_input, "fsdp", split_axis=0, concat_axis=0, tiled=True),
    )
    gathered = lax.all_gather(base_weight, "fsdp", axis=0, tiled=True)
    frozen_value_rows = jnp.dot(tokens, gathered, preferred_element_type=jnp.float32)
    frozen_input_rows = lax.dot_general(
        out_grad, gathered, contract_last, preferred_element_type=jnp.float32
    )
    own_values = home_values[slot_index]
    own_inputs = home_inputs[slot_index]
    value_output = (frozen_value_rows + own_values.astype(jnp.float32)).astype(jnp.bfloat16)
    input_gradient = (frozen_input_rows + own_inputs.astype(jnp.float32)).astype(jnp.bfloat16)
    gradient_list = gradient_list[None]
    new_first = beta_first * first_moment + (1.0 - beta_first) * gradient_list
    new_second = beta_second * second_moment + (1.0 - beta_second) * gradient_list * gradient_list
    adam_step = new_first / bias_first / (jnp.sqrt(new_second / bias_second) + adam_eps)
    new_factors = factors - learn_rate * adam_step
    return (value_output, input_gradient, new_factors, new_first, new_second)


def solution(mesh):
    placed = (
        P(("groups", "fsdp"), None),
        P(("groups", "fsdp"), None),
        P("fsdp", None),
        P(("groups", "fsdp")),
        P("groups"),
        P(("groups", "fsdp"), None, None),
        P(("groups", "fsdp"), None, None),
        P(("groups", "fsdp"), None, None),
    )
    return jax.shard_map(
        local,
        mesh=mesh,
        in_specs=placed,
        out_specs=(
            P(("groups", "fsdp"), None),
            P(("groups", "fsdp"), None),
            P(("groups", "fsdp"), None, None),
            P(("groups", "fsdp"), None, None),
            P(("groups", "fsdp"), None, None),
        ),
        check_vma=False,
    )
```

profile of v0, /device:TPU:0, one launch (start us, length us, event | category | flops | bytes accessed | tf_op | source)
XLA Modules:
  0.0 499.8 jit_solution(11549336511304291775)
XLA Ops:
  7.2 0.8 select_reduce_fusion
  8.0 0.6 reduce-window.6
  8.6 0.2 slice_reduce_fusion
  8.8 0.1 bitcast_bitcast_fusion
  8.9 1.8 scatter_custom_fusion.1
  10.7 0.9 all_to_all.38
  11.6 7.3 %all-to-all-start.2 = ((bf16[32,12,512]{2,1,0:T(8,128)(2,1)}), bf16[32,12,512]{2,1,0:T(8,128)(2,1)S(1)}, u32[]{:S(2)}, u32[]{:S(2)}) async-start(bf16[32,12,512]{2,1,0:T(8,128)(2,1)} %all_to_all.38), calls=%async_computation.2 | async-start | bytes 1048576 | tf_op jit(solution)/shard_map/all_to_all | solution.py:90
  18.9 9.7 %scatter_custom_fusion = bf16[384,8192]{1,0:T(8,128)(2,1)} fusion(s32[192]{0:T(256)S(1)} %bitcast.33, bf16[192,8192]{1,0:T(8,128)(2,1)} %param.8, bf16[]{:T(256)} %constant.15.clone.1), kind=kCustom, calls=%fused_computation.9 | custom fusion | bytes 6291968 | tf_op jit(solution)/shard_map/scatter | solution.py:83
  28.6 8.5 %all_to_all.32 = bf16[32,12,8192]{2,1,0:T(8,128)(2,1)} reshape(bf16[384,8192]{1,0:T(8,128)(2,1)} %scatter_custom_fusion) | data formatting | bytes 12582912 | tf_op jit(solution)/shard_map/all_to_all | solution.py:89
  37.2 6.0 %all-to-all-start = ((bf16[32,12,8192]{2,1,0:T(8,128)(2,1)}), bf16[32,12,8192]{2,1,0:T(8,128)(2,1)}, u32[]{:S(2)}, u32[]{:S(2)}) async-start(bf16[32,12,8192]{2,1,0:T(8,128)(2,1)} %all_to_all.32), calls=%async_computation | async-start | bytes 16777216 | tf_op jit(solution)/shard_map/all_to_all | solution.py:89
  43.2 0.7 all-gather.2.cloned.1.call-update
  43.9 0.1 all_to_all.40
  44.0 0.2 fusion.8
  44.3 4.4 multiply_convert_fusion
  48.7 8.6 %all_to_all.41 = bf16[32,12,8192]{2,1,0:T(8,128)(2,1)} reshape(bf16[384,8192]{1,0:T(8,128)(2,1)} %multiply_convert_fusion) | data formatting | bytes 12582912 | tf_op jit(solution)/shard_map/all_to_all | solution.py:108
  57.3 209.7 %all-to-all-done = bf16[32,12,8192]{2,1,0:T(8,128)(2,1)} async-done(((bf16[32,12,8192]{2,1,0:T(8,128)(2,1)}), bf16[32,12,8192]{2,1,0:T(8,128)(2,1)}, u32[]{:S(2)}, u32[]{:S(2)}) %all-to-all-start) | async-done | bytes 6291488 | tf_op jit(solution)/shard_map/all_to_all | solution.py:89
  267.0 3.9 all-to-all-start.3
  270.9 8.7 %all_to_all.34 = bf16[384,8192]{1,0:T(8,128)(2,1)} reshape(bf16[32,12,8192]{2,1,0:T(8,128)(2,1)} %all-to-all-done) | data formatting | bytes 12582912 | tf_op jit(solution)/shard_map/all_to_all | solution.py:89
  279.6 4.5 fusion.7
  284.1 0.3 fusion.4
  284.4 0.9 all_to_all.35
  285.3 0.2 fusion.6
  285.5 3.7 fusion.1
  289.2 167.8 %all-to-all-done.3 = bf16[32,12,8192]{2,1,0:T(8,128)(2,1)} async-done(((bf16[32,12,8192]{2,1,0:T(8,128)(2,1)}), bf16[32,12,8192]{2,1,0:T(8,128)(2,1)}, u32[]{:S(2)}, u32[]{:S(2)}) %all-to-all-start.3) | async-done | bytes 6291488 | tf_op jit(solution)/shard_map/all_to_all | solution.py:108
  457.0 3.3 all-to-all-start.1
  460.3 1.4 multiply_subtract_fusion
  461.7 8.7 %all_to_all.43 = bf16[384,8192]{1,0:T(8,128)(2,1)} reshape(bf16[32,12,8192]{2,1,0:T(8,128)(2,1)} %all-to-all-done.3) | data formatting | bytes 12582912 | tf_op jit(solution)/shard_map/all_to_all | solution.py:108
  470.5 9.0 %gather_fusion.1 = bf16[192,8192]{1,0:T(8,128)(2,1)S(1)} fusion(bf16[384,8192]{1,0:T(8,128)(2,1)} %all_to_all.43, s32[1024]{0:T(1024)S(1)} %pad_clamp_fusion), kind=kCustom, calls=%fused_computation.1 | custom fusion | bytes 6292224 | tf_op jit(solution)/shard_map/gather | solution.py:116
  479.5 1.1 all_to_all.37
  480.6 1.7 gather_fusion
  482.3 8.2 %fusion = bf16[192,8192]{1,0:T(8,128)(2,1)} fusion(bf16[192,512]{1,0:T(8,128)(2,1)} %param.9, bf16[8192,512]{1,0:T(8,128)(2,1)} %all-gather.2.cloned.1.call-done, bf16[192,8192]{1,0:T(8,128)(2,1)S(1)} %gather_fusion.1), kind=kOutput, calls=%fused_computation.6 | convolution fusion | flops 1615331328 | bytes 14876672 | tf_op jit(solution)/shard_map/dot_general | solution.py:112
  490.5 2.5 fusion.5
  (25 shorter events, 0.2 us)
Async XLA Ops:
  11.6 25.6 %all-to-all-start.2 = ((bf16[32,12,512]{2,1,0:T(8,128)(2,1)}), bf16[32,12,512]{2,1,0:T(8,128)(2,1)S(1)}, u32[]{:S(2)}, u32[]{:S(2)}) async-start(bf16[32,12,512]{2,1,0:T(8,128)(2,1)} %all_to_all.38), calls=%async_computation.2 | async-start | bytes 1048576 | tf_op jit(solution)/shard_map/all_to_all | solution.py:90
  37.2 6.7 %copy-start.1 = (f32[1,16,8704]{2,1,0:T(8,128)S(1)}, f32[1,16,8704]{2,1,0:T(8,128)}, u32[]{:S(2)}) copy-start(f32[1,16,8704]{2,1,0:T(8,128)} %param.13) | copy-start | bytes 1671172
  37.2 229.8 %all-to-all-start = ((bf16[32,12,8192]{2,1,0:T(8,128)(2,1)}), bf16[32,12,8192]{2,1,0:T(8,128)(2,1)}, u32[]{:S(2)}, u32[]{:S(2)}) async-start(bf16[32,12,8192]{2,1,0:T(8,128)(2,1)} %all_to_all.32), calls=%async_computation | async-start | bytes 16777216 | tf_op jit(solution)/shard_map/all_to_all | solution.py:89
  43.2 439.1 %all-gather.2.cloned.1.call-start = ((), (), s32[]{:S(2)}) async-start(), calls=%async_computation.4 | async-start | bytes 8650752 | tf_op jit(solution)/shard_map/all_gather | solution.py:110
  267.0 190.0 %all-to-all-start.3 = ((bf16[32,12,8192]{2,1,0:T(8,128)(2,1)}), bf16[32,12,8192]{2,1,0:T(8,128)(2,1)}, u32[]{:S(2)}, u32[]{:S(2)}) async-start(bf16[32,12,8192]{2,1,0:T(8,128)(2,1)} %all_to_all.41), calls=%async_computation.3 | async-start | bytes 16777216 | tf_op jit(solution)/shard_map/all_to_all | solution.py:108
  284.1 176.2 %copy-start.2 = (f32[1,16,8704]{2,1,0:T(8,128)S(1)}, f32[1,16,8704]{2,1,0:T(8,128)}, u32[]{:S(2)}) copy-start(f32[1,16,8704]{2,1,0:T(8,128)} %param.14) | copy-start | bytes 1671172
  284.1 176.2 %copy-start.3 = (f32[1,16,8704]{2,1,0:T(8,128)S(1)}, f32[1,16,8704]{2,1,0:T(8,128)}, u32[]{:S(2)}) copy-start(f32[1,16,8704]{2,1,0:T(8,128)} %param.15) | copy-start | bytes 1671172
  457.0 22.5 %all-to-all-start.1 = ((bf16[32,12,512]{2,1,0:T(8,128)(2,1)}), bf16[32,12,512]{2,1,0:T(8,128)(2,1)}, u32[]{:S(2)}, u32[]{:S(2)}) async-start(bf16[32,12,512]{2,1,0:T(8,128)(2,1)} %all_to_all.35), calls=%async_computation.1 | async-start | bytes 1048576 | tf_op jit(solution)/shard_map/all_to_all | solution.py:107
  482.3 8.2 %copy-start.4 = (bf16[192,512]{1,0:T(8,128)(2,1)S(1)}, bf16[192,512]{1,0:T(8,128)(2,1)}, u32[]{:S(2)}) copy-start(bf16[192,512]{1,0:T(8,128)(2,1)} %gather_fusion) | copy-start | bytes 589828
  482.3 8.2 %copy-start = (bf16[8192,512]{1,0:T(8,128)(2,1)S(1)}, bf16[8192,512]{1,0:T(8,128)(2,1)}, u32[]{:S(2)}) copy-start(bf16[8192,512]{1,0:T(8,128)(2,1)} %all-gather.2.cloned.1.call-done) | copy-start | bytes 25165828
  482.3 8.2 %copy-start.5 = (bf16[192,8192]{1,0:T(8,128)(2,1)S(1)}, bf16[192,8192]{1,0:T(8,128)(2,1)}, u32[]{:S(2)}) copy-start(bf16[192,8192]{1,0:T(8,128)(2,1)} %param.8) | copy-start | bytes 9437188
Sparse Core Ops, SparseCore 0:
  46.9 154.7 all-gather.1
where the time goes:
time: 501 us; the launch traced here: 500 us
  waiting for transfers between devices  378 us (75%)
  local copies, waits for them, and re-layouts  60 us (12%)
  matrix products  24 us (5%)
  starting transfers between devices  20.5 us (4%)
  between operations  14.2 us (3%)
    all_to_all x1, waiting for transfers between devices, local(): lax.all_to_all(send_tokens, 'fsdp', split_axis=0, concat_axis=0, tiled=True)  210 us
    all_to_all x1, waiting for transfers between devices, local(): lax.all_to_all(adapter_input, 'fsdp', split_axis=0, concat_axis=0, tiled=...  168 us
    all_to_all x2, local copies, waits for them, and re-layouts, local(): lax.all_to_all(adapter_input, 'fsdp', split_axis=0, concat_axis=0, tiled=...  17.4 us
    all_to_all x2, local copies, waits for them, and re-layouts, local(): lax.all_to_all(send_tokens, 'fsdp', split_axis=0, concat_axis=0, tiled=True)  17.3 us
  transfers between devices with their start and end apart: 5, of which 2 were waited for; matrix products, arithmetic and copies ran while one was open for 7% of the time, Pallas kernels for 0%

commit v1 on v0

v1 whole, which is shorter than its diff:
```python
import math

import jax
import jax.numpy as jnp
from jax import lax
from jax.sharding import PartitionSpec as P

adapter_scale = 0.25
beta_first = 0.9
beta_second = 0.95
adam_eps = 1e-08
learn_rate = 0.05
bias_first = 0.271
bias_second = 0.142625
contract_last = (((1,), (1,)), ((), ()))
contract_first = (((0,), (0,)), ((), ()))


def local(
    tokens, out_grad, base_weight, adapter_ids, adapter_home, factors, first_moment, second_moment
):
    tok_count, feature_width = tokens.shape
    devices = lax.axis_size("fsdp")
    rank = factors.shape[1]
    input_scale = 1.0 / math.sqrt(feature_width)
    compute = factors[0].astype(jnp.bfloat16)
    up_all = lax.all_gather(compute[:, feature_width:], "fsdp", axis=0, tiled=True)
    down_all = lax.all_gather(compute[:, :feature_width], "fsdp", axis=0, tiled=True)
    weight = lax.all_gather(base_weight, "fsdp", axis=0, tiled=True)

    columns = jnp.arange(devices, dtype=jnp.int32)
    adapter_hot = (adapter_ids[:, None] == columns[None, :]).astype(jnp.int32)
    target = jnp.sum(adapter_hot * adapter_home[None, :], axis=1)
    mask = target[:, None] == jnp.arange(devices * rank, dtype=jnp.int32)[None, :] // rank

    def masked(x):
        return jnp.where(mask, x, 0.0).astype(jnp.bfloat16)

    low_grad = masked(
        adapter_scale
        * lax.dot_general(out_grad, up_all, contract_last, preferred_element_type=jnp.float32)
    )
    down_grad = (
        input_scale
        * lax.dot_general(low_grad, tokens, contract_first, preferred_element_type=jnp.float32)
    ).astype(jnp.bfloat16)
    down_sum = lax.psum_scatter(down_grad, "fsdp", scatter_dimension=0, tiled=True)
    projected = masked(
        input_scale
        * lax.dot_general(tokens, down_all, contract_last, preferred_element_type=jnp.float32)
    )
    up_grad = adapter_scale * lax.dot_general(
        projected, out_grad, contract_first, preferred_element_type=jnp.float32
    )
    up_sum = lax.psum_scatter(up_grad, "fsdp", scatter_dimension=0, tiled=True)
    own_values = (
        adapter_scale * jnp.dot(projected, up_all, preferred_element_type=jnp.float32)
    ).astype(jnp.bfloat16)
    own_inputs = (
        input_scale * jnp.dot(low_grad, down_all, preferred_element_type=jnp.float32)
    ).astype(jnp.bfloat16)
    frozen_value_rows = jnp.dot(tokens, weight, preferred_element_type=jnp.float32)
    frozen_input_rows = lax.dot_general(
        out_grad, weight, contract_last, preferred_element_type=jnp.float32
    )
    value_output = (frozen_value_rows + own_values.astype(jnp.float32)).astype(jnp.bfloat16)
    input_gradient = (frozen_input_rows + own_inputs.astype(jnp.float32)).astype(jnp.bfloat16)
    gradient_list = jnp.concatenate([down_sum.astype(jnp.float32), up_sum], axis=1)[None]
    new_first = beta_first * first_moment + (1.0 - beta_first) * gradient_list
    new_second = beta_second * second_moment + (1.0 - beta_second) * gradient_list * gradient_list
    adam_step = new_first / bias_first / (jnp.sqrt(new_second / bias_second) + adam_eps)
    new_factors = factors - learn_rate * adam_step
    return (value_output, input_gradient, new_factors, new_first, new_second)


def solution(mesh):
    placed = (
        P(("groups", "fsdp"), None),
        P(("groups", "fsdp"), None),
        P("fsdp", None),
        P(("groups", "fsdp")),
        P("groups"),
        P(("groups", "fsdp"), None, None),
        P(("groups", "fsdp"), None, None),
        P(("groups", "fsdp"), None, None),
    )
    return jax.shard_map(
        local,
        mesh=mesh,
        in_specs=placed,
        out_specs=(
            P(("groups", "fsdp"), None),
            P(("groups", "fsdp"), None),
            P(("groups", "fsdp"), None, None),
            P(("groups", "fsdp"), None, None),
            P(("groups", "fsdp"), None, None),
        ),
        check_vma=False,
    )
```

time: 501 us -> 464 us (0.926)
  local copies, waits for them, and re-layouts: 60 us -> 1.54 us
  blocking collectives: 0 us -> 45.9 us
  starting transfers between devices: 20.5 us -> 0.16 us
  waiting for transfers between devices: 378 us -> 358 us
  matrix products: 24 us -> 36.8 us
    all_to_all x4 -> x0, waiting for transfers between devices: 377 us -> none  [the longest x1 210 us: local(): lax.all_to_all(send_tokens, 'fsdp', split_axis=0, concat_axis=0, tiled=True)]
    reduce_scatter x0 -> x2, waiting for transfers between devices: none -> 268 us  [the longest x1 137 us: local(): lax.psum_scatter(down_grad, 'fsdp', scatter_dimension=0, tiled=True)]
    all_gather x1 -> x2, waiting for transfers between devices: 0.01 us -> 89.5 us  [the longest x1 62.1 us: local(): weight = lax.all_gather(base_weight, 'fsdp', axis=0, tiled=True)]
    all_gather x0 -> x1, blocking collectives: none -> 45.9 us  [local(): lax.all_gather(compute[:, feature_width:], 'fsdp', axis=0, tiled=True)]
    all_to_all x8 -> x0, local copies, waits for them, and re-layouts: 37.6 us -> none  [the longest x2 17.4 us: local(): lax.all_to_all(adapter_input, 'fsdp', split_axis=0, concat_axis=0, tiled=...]
    all_to_all x4 -> x0, starting transfers between devices: 20.5 us -> none  [the longest x1 7.3 us: local(): lax.all_to_all(send_grads, 'fsdp', split_axis=0, concat_axis=0, tiled=True)]
    dot_general x8, matrix products: 24 us -> 36.8 us  [the longest x1 9.85 us: local(): lax.dot_general(out_grad, weight, contract_last, preferred_element_type=j...]
    scatter x2 -> x0, local copies, waits for them, and re-layouts: 11.5 us -> none  [the longest x1 9.72 us: local(): jnp.zeros((devices * capacity, feature_width), jnp.bfloat16).at[slot_index]]
  transfers between devices with their start and end apart: 5 -> 4, of which waited for: 2 -> 4; matrix products, arithmetic and copies ran while one was open for 7% -> 8% of each run, Pallas kernels for 0% -> 0%
where the time goes in v1:
time: 464 us; the launch traced here: 463 us
  waiting for transfers between devices  358 us (77%)
  blocking collectives  45.9 us (10%)
  matrix products  36.8 us (8%)
  between operations  13.8 us (3%)
  other arithmetic  6.75 us (1%)
    reduce_scatter x1, waiting for transfers between devices, local(): lax.psum_scatter(down_grad, 'fsdp', scatter_dimension=0, tiled=True)  137 us
    reduce_scatter x1, waiting for transfers between devices, local(): up_sum = lax.psum_scatter(up_grad, 'fsdp', scatter_dimension=0, tiled=True)  131 us
    all_gather x1, waiting for transfers between devices, local(): weight = lax.all_gather(base_weight, 'fsdp', axis=0, tiled=True)  62.1 us
    all_gather x1, blocking collectives, local(): lax.all_gather(compute[:, feature_width:], 'fsdp', axis=0, tiled=True)  45.9 us
    all_gather x1, waiting for transfers between devices, local(): lax.all_gather(compute[:, :feature_width], 'fsdp', axis=0, tiled=True)  27.4 us
    dot_general x1, matrix products, local(): lax.dot_general(out_grad, weight, contract_last, preferred_element_type=j...  9.85 us
  transfers between devices with their start and end apart: 4, of which 4 were waited for; matrix products, arithmetic and copies ran while one was open for 8% of the time, Pallas kernels for 0%

profile of v1, /device:TPU:0, one launch (start us, length us, event | category | flops | bytes accessed | tf_op | source)
XLA Modules:
  0.0 463.3 jit_solution(2301065198393927530)
XLA Ops:
  7.2 0.0 copy-start
  7.2 0.0 all-gather.5.cloned.1.call-start
  7.2 1.2 convert_bitcast_fusion
  8.5 0.7 slice.8
  9.2 0.0 all-gather.5.cloned.1.call-update
  9.2 0.0 all-gather.3.cloned.1.call-start
  9.3 0.7 all-gather.3.cloned.1.call-update
  10.0 0.0 reduce-scatter.3.cloned.1.call-start
  10.0 0.8 select_reduce_fusion
  10.8 45.9 %all_gather.11 = bf16[512,512]{1,0:T(8,128)(2,1)S(1)} all-gather(bf16[16,512]{1,0:T(8,128)(2,1)S(1)} %slice.9), channel_id=1, replica_groups=mesh['groups'=1,'fsdp'=32] {'fsdp'}, dimensions={0}, use_global_device_ids=true | all-gather | bytes 540672 | tf_op jit(solution)/shard_map/all_gather | solution.py:27
  56.7 0.8 copy-done.2
  57.5 1.3 fusion.5
  58.7 0.0 copy-done
  58.7 6.3 %multiply_convert_fusion = bf16[512,8192]{1,0:T(8,128)(2,1)} fusion(bf16[192,512]{1,0:T(8,128)(2,1)S(1)} %fusion.5, bf16[192,8192]{1,0:T(8,128)(2,1)S(1)} %copy-done), kind=kOutput, calls=%fused_computation | convolution fusion | flops 1619001344 | bytes 11730944 | tf_op jit(solution)/shard_map/dot_general | solution.py:45
  65.1 0.0 reduce-scatter.3.cloned.1.call-update
  65.1 0.0 copy-start.4
  65.1 0.0 reduce-scatter.5.cloned.1.call-start
  65.1 27.4 %all-gather.5.cloned.1.call-done = bf16[512,8192]{1,0:T(8,128)(2,1)} async-done(((bf16[16,8192]{1,0:T(8,128)(2,1)}), bf16[512,8192]{1,0:T(8,128)(2,1)}) %all-gather.5.cloned.1.call-update) | async-done | bytes 8388624 | tf_op jit(solution)/shard_map/all_gather | solution.py:28
  92.5 6.3 %fusion.9 = bf16[192,512]{1,0:T(8,128)(2,1)S(1)} fusion(bf16[192,8192]{1,0:T(8,128)(2,1)S(1)} %copy-done, bf16[512,8192]{1,0:T(8,128)(2,1)} %all-gather.5.cloned.1.call-done, s32[512]{0:T(512)S(1)} %add_select_fusion, s32[192]{0:T(256)S(1)} %select_reduce_fusion), kind=kOutput, calls=%fused_computation.17 | convolution fusion | flops 1611005952 | bytes 11733760 | tf_op jit(solution)/shard_map/dot_general | solution.py:50
  98.9 0.0 copy-done.3
  98.9 1.0 fusion.7
  99.9 1.3 convolution_multiply_fusion.1
  101.2 0.0 reduce-scatter.5.cloned.1.call-update
  101.3 8.1 %fusion.2 = f32[192,8192]{1,0:T(8,128)} fusion(bf16[192,512]{1,0:T(8,128)(2,1)S(1)} %fusion.5, bf16[512,8192]{1,0:T(8,128)(2,1)} %all-gather.5.cloned.1.call-done), kind=kOutput, calls=%fused_computation.5 | convolution fusion | flops 1615331328 | bytes 14876672 | tf_op jit(solution)/shard_map/dot_general | solution.py:60
  109.4 62.1 %all-gather.3.cloned.1.call-done = bf16[8192,512]{1,0:T(8,128)(2,1)} async-done(((bf16[256,512]{1,0:T(8,128)(2,1)}), bf16[8192,512]{1,0:T(8,128)(2,1)}) %all-gather.3.cloned.1.call-update) | async-done | bytes 8388624 | tf_op jit(solution)/shard_map/all_gather | solution.py:29
  171.5 9.8 %fusion = bf16[192,8192]{1,0:T(8,128)(2,1)} fusion(f32[192,8192]{1,0:T(8,128)} %fusion.2, bf16[192,512]{1,0:T(8,128)(2,1)S(1)} %copy-done.4, bf16[8192,512]{1,0:T(8,128)(2,1)} %all-gather.3.cloned.1.call-done), kind=kOutput, calls=%fused_computation.3 | convolution fusion | flops 1613758464 | bytes 18022400 | tf_op jit(solution)/shard_map/dot_general | solution.py:63
  181.3 0.0 copy-done.5
  181.3 2.5 fusion.8
  183.9 137.1 %reduce-scatter.3.cloned.1.call-done = bf16[16,8192]{1,0:T(8,128)(2,1)} async-done(((bf16[512,8192]{1,0:T(8,128)(2,1)}), bf16[16,8192]{1,0:T(8,128)(2,1)}) %reduce-scatter.3.cloned.1.call-update) | async-done | bytes 262160 | tf_op jit(solution)/shard_map/reduce_scatter | solution.py:47
  320.9 1.8 bitcast_convert_fusion
  322.7 131.1 %reduce-scatter.5.cloned.1.call-done = f32[16,512]{1,0:T(8,128)} async-done(((f32[512,512]{1,0:T(8,128)}), f32[16,512]{1,0:T(8,128)}) %reduce-scatter.5.cloned.1.call-update) | async-done | bytes 32784 | tf_op jit(solution)/shard_map/reduce_scatter | solution.py:55
  453.8 3.0 multiply_subtract_fusion
  (8 shorter events, 0.0 us)
Async XLA Ops:
  7.2 51.6 %copy-start = (bf16[192,8192]{1,0:T(8,128)(2,1)S(1)}, bf16[192,8192]{1,0:T(8,128)(2,1)}, u32[]{:S(2)}) copy-start(bf16[192,8192]{1,0:T(8,128)(2,1)} %param.8) | copy-start | bytes 9437188
  7.2 85.4 %all-gather.5.cloned.1.call-start = ((), (), s32[]{:S(2)}) async-start(), calls=%async_computation.3 | async-start | bytes 8650752 | tf_op jit(solution)/shard_map/all_gather | solution.py:28
  9.2 162.3 %all-gather.3.cloned.1.call-start = ((), (), s32[]{:S(2)}) async-start(), calls=%async_computation.2 | async-start | bytes 8650752 | tf_op jit(solution)/shard_map/all_gather | solution.py:29
  10.0 311.0 %reduce-scatter.3.cloned.1.call-start = ((), (), s32[]{:S(2)}) async-start(), calls=%async_computation.4 | async-start | bytes 8650752 | tf_op jit(solution)/shard_map/reduce_scatter | solution.py:47
  56.7 0.8 copy-start.2
  65.1 34.8 %copy-start.4 = (bf16[192,512]{1,0:T(8,128)(2,1)S(1)}, bf16[192,512]{1,0:T(8,128)(2,1)}, u32[]{:S(2)}) copy-start(bf16[192,512]{1,0:T(8,128)(2,1)} %param.9) | copy-start | bytes 589828
  65.1 388.7 %reduce-scatter.5.cloned.1.call-start = ((), (), s32[]{:S(2)}) async-start(), calls=%async_computation.5 | async-start | bytes 1081344 | tf_op jit(solution)/shard_map/reduce_scatter | solution.py:55
  92.5 6.4 %copy-start.3 = (bf16[512,512]{1,0:T(8,128)(2,1)S(1)}, bf16[512,512]{1,0:T(8,128)(2,1)}, u32[]{:S(2)}) copy-start(bf16[512,512]{1,0:T(8,128)(2,1)} %copy-done.2) | copy-start | bytes 1572868
  171.5 9.9 %copy-start.1 = (bf16[8192,512]{1,0:T(8,128)(2,1)S(1)}, bf16[8192,512]{1,0:T(8,128)(2,1)}, u32[]{:S(2)}) copy-start(bf16[8192,512]{1,0:T(8,128)(2,1)} %all-gather.3.cloned.1.call-done) | copy-start | bytes 25165828
  171.5 9.9 %copy-start.5 = (f32[192,512]{1,0:T(8,128)S(1)}, f32[192,512]{1,0:T(8,128)}, u32[]{:S(2)}) copy-start(f32[192,512]{1,0:T(8,128)} %fusion.7) | copy-start | bytes 1179652
Sparse Core Ops, SparseCore 0:
  11.5 81.0 all-gather.4
  95.4 76.0 all-gather.2
  173.8 147.1 reduce-scatter.2
  323.0 130.7 reduce-scatter.4

commit v2 on v1

v2 whole, which is shorter than its diff:
```python
import functools
import math

import jax
import jax.numpy as jnp
from jax import lax
from jax.experimental import pallas as pl
from jax.experimental.pallas import tpu as pltpu
from jax.sharding import PartitionSpec as P

adapter_scale = 0.25
beta_first = 0.9
beta_second = 0.95
adam_eps = 1e-08
learn_rate = 0.05
bias_first = 0.271
bias_second = 0.142625
contract_last = (((1,), (1,)), ((), ()))
contract_first = (((0,), (0,)), ((), ()))
f32 = jnp.float32
bf16 = jnp.bfloat16
vmem_bytes = 48 * 2**20


def dot(a, b, dims=(((1,), (0,)), ((), ()))):
    return lax.dot_general(a, b, dims, preferred_element_type=f32)


class Plan:
    def __init__(self, devices):
        self.devices = devices
        self.chips = devices // 2
        bits = self.chips.bit_length() - 1
        self.basis = (1, 2, 4, 12) if self.chips == 16 else tuple(1 << i for i in range(bits))
        self.bits = bits

    def order(self, stream, core):
        turn = (self.bits // 2 if stream == "d" else 0) + core
        return tuple(self.basis[(i + turn) % self.bits] for i in range(self.bits))

    def masks(self, stream, core):
        order = self.order(stream, core)
        out = []
        for b in range(self.chips):
            m = 0
            for i, flip in enumerate(order):
                if b >> i & 1:
                    m ^= flip
            out.append(m)
        return out

    def by_core(self, core, stream):
        return jnp.where(
            core == 0,
            jnp.array(self.masks(stream, 0), jnp.int32),
            jnp.array(self.masks(stream, 1), jnp.int32),
        )

    def swap(self, x):
        return lax.ppermute(x, "fsdp", [(i, i ^ 1) for i in range(self.devices)])

    def step(self, x, stream, i):
        pairs = []
        for d in range(self.devices):
            flip = self.order(stream, d & 1)[i]
            pairs.append((d, ((d >> 1) ^ flip) << 1 | (d & 1)))
        return lax.ppermute(x, "fsdp", pairs)


whole_vmem = pl.BlockSpec(memory_space=pltpu.VMEM)
anywhere = pl.BlockSpec(memory_space=pl.ANY)


def params():
    return pltpu.CompilerParams(vmem_limit_bytes=vmem_bytes)


def join_kernel(count, *refs):
    for i in range(count):
        own, got, out = refs[2 * i], refs[2 * i + 1], refs[2 * count + i]
        rows = own.shape[0]
        out[:rows] = own[...]
        out[rows:] = got[...]


def join(pairs):
    count = len(pairs)
    flat = [x for pair in pairs for x in pair]
    return pl.pallas_call(
        functools.partial(join_kernel, count),
        in_specs=[whole_vmem] * (2 * count),
        out_specs=[whole_vmem] * count,
        out_shape=[jax.ShapeDtypeStruct((2 * x.shape[0], x.shape[1]), x.dtype) for x, _ in pairs],
        compiler_params=params(),
        cost_estimate=pl.CostEstimate(
            flops=0, bytes_accessed=4 * sum(x.size for x in flat), transcendentals=0
        ),
    )(*flat)


def fold_kernel(count, *refs):
    for i in range(count):
        keep, got = refs[2 * i], refs[2 * i + 1]
        kept, sent = refs[2 * count + 2 * i], refs[2 * count + 2 * i + 1]
        half = kept.shape[0]
        kept[...] = (keep[:half].astype(f32) + got[:half].astype(f32)).astype(kept.dtype)
        sent[...] = (keep[half:].astype(f32) + got[half:].astype(f32)).astype(sent.dtype)


def fold(pairs):
    count = len(pairs)
    flat = [x for pair in pairs for x in pair]
    shapes = [
        jax.ShapeDtypeStruct((x.shape[0] // 2, x.shape[1]), x.dtype) for x, _ in pairs for _ in "ks"
    ]
    out = pl.pallas_call(
        functools.partial(fold_kernel, count),
        in_specs=[whole_vmem] * (2 * count),
        out_specs=[whole_vmem] * (2 * count),
        out_shape=shapes,
        compiler_params=params(),
        cost_estimate=pl.CostEstimate(
            flops=sum(x.size for x in flat),
            bytes_accessed=4 * sum(x.size for x in flat),
            transcendentals=0,
        ),
    )(*flat)
    return [(out[2 * i], out[2 * i + 1]) for i in range(count)]


def tie_kernel(*refs):
    del refs


def tie(arrays, after):
    count = len(arrays)
    return pl.pallas_call(
        tie_kernel,
        in_specs=[anywhere] * (count + len(after)),
        out_specs=[anywhere] * count,
        out_shape=[jax.ShapeDtypeStruct(x.shape, x.dtype) for x in arrays],
        input_output_aliases={i: i for i in range(count)},
        cost_estimate=pl.CostEstimate(flops=0, bytes_accessed=0, transcendentals=0),
    )(*arrays, *after)


def factor_kernel(width, wide, info, f_ref, own_ref, send_ref):
    core = info[0]
    blocks = wide // width
    for i in range(blocks // 2):
        mine = pl.multiple_of((2 * i + core) * width, width)
        other = pl.multiple_of((2 * i + 1 - core) * width, width)
        own_ref[:, i * width : (i + 1) * width] = f_ref[:, pl.ds(mine, width)].astype(bf16)
        send_ref[:, i * width : (i + 1) * width] = f_ref[:, pl.ds(other, width)].astype(bf16)
    up = f_ref[:, wide:].astype(bf16)
    own_ref[:, wide // 2 :] = up
    send_ref[:, wide // 2 :] = up


def split_factors(info, factors, width, wide):
    rank, total = factors.shape
    shape = jax.ShapeDtypeStruct((rank, wide // 2 + total - wide), bf16)
    return pl.pallas_call(
        functools.partial(factor_kernel, width, wide),
        in_specs=[pl.BlockSpec(memory_space=pltpu.SMEM), pl.BlockSpec(memory_space=pltpu.VMEM)],
        out_specs=[pl.BlockSpec(memory_space=pltpu.VMEM)] * 2,
        out_shape=[shape, shape],
        cost_estimate=pl.CostEstimate(flops=0, bytes_accessed=1_000_000, transcendentals=0),
    )(info, factors)


def join_factors_kernel(half, own_ref, got_ref, up_ref, down_ref):
    rank = own_ref.shape[0]
    for at, ref in ((0, own_ref), (rank, got_ref)):
        down_ref[at : at + rank] = ref[:, :half]
        up_ref[at : at + rank] = ref[:, half:]


def join_factors(own, got, half):
    rank, total = own.shape
    return pl.pallas_call(
        functools.partial(join_factors_kernel, half),
        in_specs=[whole_vmem] * 2,
        out_specs=[whole_vmem] * 2,
        out_shape=[
            jax.ShapeDtypeStruct((2 * rank, total - half), bf16),
            jax.ShapeDtypeStruct((2 * rank, half), bf16),
        ],
        cost_estimate=pl.CostEstimate(flops=0, bytes_accessed=8 * rank * total, transcendentals=0),
    )(own, got)


def halves_kernel(width, info, x_ref, own_ref, other_ref):
    core = info[0]
    for i in range(own_ref.shape[1] // width):
        mine = pl.multiple_of((2 * i + core) * width, width)
        other = pl.multiple_of((2 * i + 1 - core) * width, width)
        at = slice(i * width, (i + 1) * width)
        own_ref[:, at] = x_ref[:, pl.ds(mine, width)]
        other_ref[:, at] = x_ref[:, pl.ds(other, width)]


def halves(info, x, width):
    rows, wide = x.shape
    step = rows // 4
    small = pl.BlockSpec((step, wide // 2), lambda i, s: (i, 0))
    return pl.pallas_call(
        functools.partial(halves_kernel, width),
        grid_spec=pltpu.PrefetchScalarGridSpec(
            num_scalar_prefetch=1,
            grid=(4,),
            in_specs=[pl.BlockSpec((step, wide), lambda i, s: (i, 0))],
            out_specs=[small, small],
        ),
        out_shape=[jax.ShapeDtypeStruct((rows, wide // 2), bf16)] * 2,
        cost_estimate=pl.CostEstimate(flops=0, bytes_accessed=rows * wide * 4, transcendentals=0),
    )(info, x)


def down_grad_kernel(half, scale, low_ref, low_two_ref, x_ref, y_ref, ka, sa, kb, sb):
    q = pl.program_id(0)
    n = x_ref.shape[0]

    def one(low, keep, send):
        out = dot(low[:, :n], x_ref[...]) + dot(low[:, n:], y_ref[...])
        out = (scale * out).astype(bf16)
        cut = out.shape[0] // 2
        keep[...] = out[:cut]
        send[...] = out[cut:]

    @pl.when(q < half)
    def _():
        one(low_ref, ka, sa)

    @pl.when(q >= half)
    def _():
        one(low_two_ref, kb, sb)


def down_grads(low, low_two, own, sibling, scale):
    rows, cols = sibling.shape
    blocks = 8
    width = cols // blocks
    half = blocks // 2
    n = low.shape[0]
    whole = pl.BlockSpec(low.shape, lambda q: (0, 0))
    part = pl.BlockSpec((rows, width), lambda q: (0, q))
    first = pl.BlockSpec((n // 2, width), lambda q: (0, jnp.minimum(q, half - 1)))
    second = pl.BlockSpec((n // 2, width), lambda q: (0, jnp.maximum(q - half, 0)))
    out = jax.ShapeDtypeStruct((n // 2, cols // 2), bf16)
    return pl.pallas_call(
        functools.partial(down_grad_kernel, half, scale),
        grid=(blocks,),
        in_specs=[whole, whole, part, part],
        out_specs=[first, first, second, second],
        out_shape=[out] * 4,
        compiler_params=params(),
        cost_estimate=pl.CostEstimate(
            flops=4 * rows * cols * n, bytes_accessed=4 * rows * cols + 2 * n * cols, transcendentals=0
        ),
    )(low, low_two, own, sibling)


def project_kernel(rank, x_ref, y_ref, a_ref, owner_ref, target_ref, add_ref, o_ref, acc):
    q = pl.program_id(0)

    @pl.when(q == 0)
    def _():
        acc[...] = jnp.zeros_like(acc)

    n = x_ref.shape[0]
    acc[:n] += dot(x_ref[...], a_ref[...], contract_last)
    acc[n:] += dot(y_ref[...], a_ref[...], contract_last)

    @pl.when(q == pl.num_programs(0) - 1)
    def _():
        kept = jnp.where(target_ref[...] == owner_ref[...], acc[...], 0.0)
        out = kept[:, :128]
        for i in range(1, kept.shape[1] // 128):
            out = out + kept[:, i * 128 : (i + 1) * 128]
        turn = rank
        while turn < 128:
            out = out + pltpu.roll(out, turn, 1)
            turn *= 2
        o_ref[...] = add_ref[...] + out


def project(own, sibling, down, owner, targets, add, rank):
    rows, cols = sibling.shape
    n = down.shape[0]
    width = cols // 4
    part = pl.BlockSpec((rows, width), lambda q: (0, q))
    still = lambda q: (0, 0)
    return pl.pallas_call(
        functools.partial(project_kernel, rank),
        grid=(4,),
        in_specs=[
            part,
            part,
            pl.BlockSpec((n, width), lambda q: (0, q)),
            pl.BlockSpec((1, n), still),
            pl.BlockSpec((2 * rows, 1), still),
            pl.BlockSpec((2 * rows, 128), still),
        ],
        out_specs=pl.BlockSpec((2 * rows, 128), still),
        out_shape=jax.ShapeDtypeStruct((2 * rows, 128), f32),
        scratch_shapes=[pltpu.VMEM((2 * rows, n), f32)],
        compiler_params=params(),
        cost_estimate=pl.CostEstimate(
            flops=4 * rows * cols * n, bytes_accessed=(4 * rows + 2 * n) * cols, transcendentals=0
        ),
    )(own, sibling, down, owner, targets, add)


def frozen_kernel(half, width, scale, info, *refs):
    x0, x1, y0, y1, a0, a1, b0, b1, u_ref, w_ref, g_ref, low_ref, v_ref, o_ref, t_ref = refs
    b = pl.program_id(0)

    @pl.when(b == 0)
    def _():
        v_ref[...] = jnp.zeros_like(v_ref)

    n = x0.shape[0]
    cut = a0.shape[0]
    v_ref[:n] += dot(x0[...], u_ref[...]) + dot(x1[...], w_ref[...])
    v_ref[n:] += dot(y0[...], u_ref[...]) + dot(y1[...], w_ref[...])
    for part, one, two, rows in ((0, a0, b0, u_ref), (half, a1, b1, w_ref)):
        lora = scale * (dot(low_ref[:, :cut], one[...]) + dot(low_ref[:, cut:], two[...]))
        out = dot(g_ref[...], rows[...], contract_last) + lora.astype(bf16).astype(f32)
        out = out.astype(bf16)
        at = pl.ds(pl.multiple_of(info[1 + part + b] * width, width), width)
        o_ref[:, at] = out[:n]
        t_ref[:, at] = out[n:]


def frozen(info, own, sibling, grads, low, down_a, down_b, weight_a, weight_b, width, scale):
    rows, cols = sibling.shape
    half = cols // width // 2
    n = down_a.shape[0]
    kv = grads.shape[1]
    still = lambda b, s: (0, 0)
    early = lambda b, s: (0, s[1 + b])
    late = lambda b, s: (0, s[1 + half + b])
    return pl.pallas_call(
        functools.partial(frozen_kernel, half, width, scale),
        grid_spec=pltpu.PrefetchScalarGridSpec(
            num_scalar_prefetch=1,
            grid=(half,),
            in_specs=[pl.BlockSpec((rows, width), early), pl.BlockSpec((rows, width), late)] * 2
            + [pl.BlockSpec((n, width), early), pl.BlockSpec((n, width), late)] * 2
            + [pl.BlockSpec((width, kv), lambda b, s: (b, 0))] * 2
            + [pl.BlockSpec((2 * rows, kv), still), pl.BlockSpec((2 * rows, 2 * n), still)],
            out_specs=[
                pl.BlockSpec((2 * rows, kv), still),
                pl.BlockSpec((rows, cols), still),
                pl.BlockSpec((rows, cols), still),
            ],
        ),
        out_shape=[
            jax.ShapeDtypeStruct((2 * rows, kv), f32),
            jax.ShapeDtypeStruct((rows, cols), bf16),
            jax.ShapeDtypeStruct((rows, cols), bf16),
        ],
        compiler_params=params(),
        cost_estimate=pl.CostEstimate(
            flops=8 * rows * cols * (n + kv),
            bytes_accessed=(8 * rows + 4 * n + 2 * kv) * cols,
            transcendentals=0,
        ),
    )(info, own, own, sibling, sibling, down_a, down_a, down_b, down_b, weight_a, weight_b, grads, low)


def merge_kernel(width, info, own_ref, got_ref, o_ref):
    core = info[0]
    for i in range(own_ref.shape[1] // width):
        mine = pl.multiple_of((2 * i + core) * width, width)
        other = pl.multiple_of((2 * i + 1 - core) * width, width)
        at = slice(i * width, (i + 1) * width)
        o_ref[:, pl.ds(mine, width)] = own_ref[:, at]
        o_ref[:, pl.ds(other, width)] = got_ref[:, at]


def merge(info, own, got, width):
    rows, cols = own.shape
    step = rows // 4
    small = pl.BlockSpec((step, cols), lambda i, s: (i, 0))
    return pl.pallas_call(
        functools.partial(merge_kernel, width),
        grid_spec=pltpu.PrefetchScalarGridSpec(
            num_scalar_prefetch=1,
            grid=(4,),
            in_specs=[small, small],
            out_specs=pl.BlockSpec((step, 2 * cols), lambda i, s: (i, 0)),
        ),
        out_shape=jax.ShapeDtypeStruct((rows, 2 * cols), own.dtype),
        cost_estimate=pl.CostEstimate(flops=0, bytes_accessed=8 * rows * cols, transcendentals=0),
    )(info, own, got)


def adam_kernel(width, info, f_ref, m_ref, v_ref, own_ref, got_ref, nf_ref, nm_ref, nv_ref):
    core = info[0]
    for i in range(f_ref.shape[1] // (2 * width)):
        own = own_ref[:, i * width : (i + 1) * width]
        got = got_ref[:, i * width : (i + 1) * width]
        left = jnp.where(core == 0, own, got)
        right = jnp.where(core == 0, got, own)
        for k, g in ((2 * i, left), (2 * i + 1, right)):
            at = slice(k * width, (k + 1) * width)
            first = beta_first * m_ref[:, at] + (1.0 - beta_first) * g
            second = beta_second * v_ref[:, at] + (1.0 - beta_second) * g * g
            step = first / bias_first / (jnp.sqrt(second / bias_second) + adam_eps)
            nf_ref[:, at] = f_ref[:, at] - learn_rate * step
            nm_ref[:, at] = first
            nv_ref[:, at] = second


def adam(info, factors, first, second, own, got, width):
    shape = jax.ShapeDtypeStruct(factors.shape, f32)
    vmem = pl.BlockSpec(memory_space=pltpu.VMEM)
    return pl.pallas_call(
        functools.partial(adam_kernel, width),
        in_specs=[pl.BlockSpec(memory_space=pltpu.SMEM)] + [vmem] * 5,
        out_specs=[vmem] * 3,
        out_shape=[shape] * 3,
        compiler_params=pltpu.CompilerParams(vmem_limit_bytes=vmem_bytes),
        cost_estimate=pl.CostEstimate(
            flops=20 * factors.size, bytes_accessed=32 * factors.size, transcendentals=0
        ),
    )(info, factors, first, second, own, got)


def local(
    tokens, out_grad, base_weight, adapter_ids, adapter_home, factors, first_moment, second_moment
):
    tok_count, feature_width = tokens.shape
    value_width = out_grad.shape[1]
    rank = factors.shape[1]
    width = base_weight.shape[0]
    plan = Plan(lax.axis_size("fsdp"))
    devices, chips = plan.devices, plan.chips
    half = feature_width // 2
    input_scale = 1.0 / math.sqrt(feature_width)
    me = lax.axis_index("fsdp")
    chip, core = me >> 1, me & 1
    mask_d = plan.by_core(core, "d")
    mask_w = plan.by_core(core, "w")
    info = jnp.concatenate([core[None].astype(jnp.int32), (chip ^ mask_w).astype(jnp.int32)])
    bits = plan.bits

    own_factors, sent_factors = split_factors(info, factors[0], width, feature_width)
    weight = base_weight
    got_weight = plan.step(weight, "w", 0)
    got_factors = plan.swap(sent_factors)
    up, down = join_factors(own_factors, got_factors, half)

    columns = jnp.arange(devices, dtype=jnp.int32)
    adapter_hot = (adapter_ids[:, None] == columns[None, :]).astype(jnp.int32)
    target = jnp.sum(adapter_hot * adapter_home[None, :], axis=1)
    tail = jnp.broadcast_to(target[:, None], (tok_count, 128)).astype(bf16)
    mine = jnp.concatenate([out_grad, tail], axis=1)
    theirs = plan.swap(mine)
    own_half, sent_half = halves(info, tokens, width)
    sibling = plan.swap(sent_half)
    both = jnp.concatenate([mine, theirs], axis=0)
    grads = both[:, :value_width]
    targets = both[:, value_width : value_width + 1].astype(jnp.int32)

    for i in range(bits - 1):
        if i > 0:
            got_weight = plan.step(weight, "w", i)
        got_down = plan.step(down, "d", i)
        got_up = plan.step(up, "d", i)
        weight, down, up = join(((weight, got_weight), (down, got_down), (up, got_up)))
    up_all = jnp.concatenate([up, plan.step(up, "d", bits - 1)], axis=0)
    weight_a, weight_b = weight, plan.step(weight, "w", bits - 1)
    down_a, down_b = down, plan.step(down, "d", bits - 1)

    within = jnp.arange(2 * rank, dtype=jnp.int32) // rank
    cores = jnp.where(within == 0, core, 1 - core)

    def owner_of(mask):
        return (2 * (chip ^ mask)[:, None] + cores[None, :]).reshape(1, -1).astype(jnp.int32)

    owner = owner_of(mask_d)
    owner_two = owner_of(mask_w)
    keep = targets == owner
    places = [[plan.masks("d", c).index(m) for m in plan.masks("w", c)] for c in (0, 1)]
    where = jnp.where(core == 0, jnp.array(places[0], jnp.int32), jnp.array(places[1], jnp.int32))
    up_two = up_all.reshape(chips, 2 * rank, value_width)[where].reshape(up_all.shape)

    def low_of(up, owner):
        out = adapter_scale * dot(up, grads, contract_last)
        return jnp.where(owner.reshape(-1, 1) == targets.reshape(1, -1), out, 0.0).astype(bf16)

    low = jnp.where(keep, adapter_scale * dot(grads, up_all, contract_last), 0.0).astype(bf16)
    keep_a, send_a, keep_b, send_b = down_grads(
        low_of(up_all, owner), low_of(up_two, owner_two), own_half, sibling, input_scale
    )
    n = down_a.shape[0]
    nothing = jnp.zeros((2 * tok_count, 128), f32)
    part_a = project(own_half, sibling, down_a, owner[:, :n], targets, nothing, rank)

    send_a, send_b = tie((send_a, send_b), (weight_b, down_b))
    for i in reversed(range(bits)):
        got_a = plan.step(send_a, "d", i)
        got_b = plan.step(send_b, "w", i)
        if i > 0:
            (keep_a, send_a), (keep_b, send_b) = fold(((keep_a, got_a), (keep_b, got_b)))
    sum_a = keep_a.astype(f32) + got_a.astype(f32)
    sum_b = keep_b.astype(f32) + got_b.astype(f32)

    part = project(own_half, sibling, down_b, owner[:, n:], targets, part_a, rank)
    other = plan.swap(part)
    total = part + jnp.concatenate([other[tok_count:], other[:tok_count]], axis=0)
    repeated = jnp.tile((input_scale * total).astype(bf16), (1, keep.shape[1] // 128))
    projected = jnp.where(keep, repeated, jnp.zeros((), bf16))
    own_blocks = [
        jnp.where(
            core == 0,
            grads[:, 2 * i * width : (2 * i + 1) * width],
            grads[:, (2 * i + 1) * width : (2 * i + 2) * width],
        )
        for i in range(value_width // (2 * width))
    ]
    half_grads = jnp.concatenate(own_blocks, axis=1)
    up_grad = adapter_scale * dot(projected, half_grads, contract_first)
    cut = up_grad.shape[0] // 2
    keep_up, send_up = up_grad[:cut], up_grad[cut:]
    for i in reversed(range(bits)):
        got_up = plan.step(send_up, "d", i)
        cut = cut // 2
        if i > 0:
            send_up = keep_up[cut:] + got_up[cut:]
            keep_up = keep_up[:cut] + got_up[:cut]
    sum_up = keep_up + got_up
    own_values = (adapter_scale * dot(projected[:tok_count], up_all)).astype(bf16)

    values, own_inputs, their_inputs = frozen(
        info, own_half, sibling, grads, low, down_a, down_b, weight_a, weight_b, width, input_scale
    )
    got_values = plan.swap(values[tok_count:])
    value_output = (values[:tok_count] + got_values + own_values.astype(f32)).astype(bf16)
    input_gradient = merge(info, own_inputs, plan.swap(their_inputs), width)

    total_grad = jnp.concatenate([sum_a, sum_b, sum_up], axis=1)
    got_grad = plan.swap(total_grad[rank:])
    new_factors, new_first, new_second = adam(
        info, factors[0], first_moment[0], second_moment[0], total_grad[:rank], got_grad, width
    )
    return (value_output, input_gradient, new_factors[None], new_first[None], new_second[None])


def solution(mesh):
    placed = (
        P(("groups", "fsdp"), None),
        P(("groups", "fsdp"), None),
        P("fsdp", None),
        P(("groups", "fsdp")),
        P("groups"),
        P(("groups", "fsdp"), None, None),
        P(("groups", "fsdp"), None, None),
        P(("groups", "fsdp"), None, None),
    )
    return jax.shard_map(
        local,
        mesh=mesh,
        in_specs=placed,
        out_specs=(
            P(("groups", "fsdp"), None),
            P(("groups", "fsdp"), None),
            P(("groups", "fsdp"), None, None),
            P(("groups", "fsdp"), None, None),
            P(("groups", "fsdp"), None, None),
        ),
        check_vma=False,
    )
```

time: 464 us -> 217 us (0.47)
  waiting for transfers between devices: 358 us -> 84.4 us
  starting transfers between devices: 0.16 us -> 58.5 us
  Pallas kernels: 0 us -> 47.8 us
  blocking collectives: 45.9 us -> 0 us
  matrix products: 36.8 us -> 5.87 us
  local copies, waits for them, and re-layouts: 1.54 us -> 15 us
  between operations: 13.8 us -> 1.1 us
    reduce_scatter x2 -> x0, waiting for transfers between devices: 268 us -> none  [the longest x1 137 us: local(): lax.psum_scatter(down_grad, 'fsdp', scatter_dimension=0, tiled=True)]
    all_gather x2 -> x0, waiting for transfers between devices: 89.5 us -> none  [the longest x1 62.1 us: local(): weight = lax.all_gather(base_weight, 'fsdp', axis=0, tiled=True)]
    ppermute x0 -> x31, waiting for transfers between devices: none -> 84.4 us  [the longest x24 83.3 us: step(): return lax.ppermute(x, 'fsdp', pairs)]
    ppermute x0 -> x31, starting transfers between devices: none -> 58.5 us  [the longest x24 40.1 us: step(): return lax.ppermute(x, 'fsdp', pairs)]
    pallas_call x0 -> x16, Pallas kernels: none -> 47.8 us  [the longest x1 10.8 us: frozen(): pl.pallas_call(functools.partial(frozen_kernel, half, width, scale), grid...]
    all_gather x1 -> x0, blocking collectives: 45.9 us -> none  [local(): lax.all_gather(compute[:, feature_width:], 'fsdp', axis=0, tiled=True)]
    dot_general x8 -> x5, matrix products: 36.8 us -> 5.87 us  [dot(): return lax.dot_general(a, b, dims, preferred_element_type=f32)]
    unnamed x12 -> x51, local copies, waits for them, and re-layouts: 0.82 us -> 11.3 us
  transfers between devices with their start and end apart: 4 -> 31, of which waited for: 4 -> 11; matrix products, arithmetic and copies ran while one was open for 8% -> 6% of each run, Pallas kernels for 0% -> 20%
where the time goes in v2:
time: 217 us; the launch traced here: 216 us
  waiting for transfers between devices  84.4 us (39%)
  starting transfers between devices  58.5 us (27%)
  Pallas kernels  47.8 us (22%)
  local copies, waits for them, and re-layouts  15 us (7%)
  matrix products  5.87 us (3%)
  other arithmetic  2.98 us (1%)
    ppermute x24, waiting for transfers between devices, step(): return lax.ppermute(x, 'fsdp', pairs)  83.3 us
    ppermute x24, starting transfers between devices, step(): return lax.ppermute(x, 'fsdp', pairs)  40.1 us
    ppermute x7, starting transfers between devices, swap(): return lax.ppermute(x, 'fsdp', [(i, i ^ 1) for i in range(self.devices)])  18.4 us
    unnamed x51, local copies, waits for them, and re-layouts  11.3 us
    pallas_call x1, Pallas kernels, frozen(): pl.pallas_call(functools.partial(frozen_kernel, half, width, scale), grid...  10.8 us
    pallas_call x2, Pallas kernels, project(): pl.pallas_call(functools.partial(project_kernel, rank), grid=(4,), in_spe...  8.59 us
    pallas_call x1, Pallas kernels, down_grads(): pl.pallas_call(functools.partial(down_grad_kernel, half, scale), grid=(bl...  7.05 us
    dot_general x5, matrix products, dot(): return lax.dot_general(a, b, dims, preferred_element_type=f32)  5.87 us
  transfers between devices with their start and end apart: 31, of which 11 were waited for; matrix products, arithmetic and copies ran while one was open for 6% of the time, Pallas kernels for 20%

profile of v2, /device:TPU:0, one launch (start us, length us, event | category | flops | bytes accessed | tf_op | source)
XLA Modules:
  0.0 215.7 jit_solution(17436537649883301003)
XLA Ops:
  1.9 1.8 shard_map.174
  4.2 2.5 %collective-permute-start.1 = (bf16[256,512]{1,0:T(8,128)(2,1)}, bf16[256,512]{1,0:T(8,128)(2,1)S(1)}, u32[]{:S(2)}, u32[]{:S(2)}) collective-permute-start(bf16[256,512]{1,0:T(8,128)(2,1)} %refs_0_.1), channel_id=1, source_target_pairs={{0,2},{1,5},{2,0},{3,7},{4,6},{5,1},{6,4},{7,3},{8,10},{9,13},{10,... | collective-permute-start | bytes 786440 | tf_op jit(solution)/shard_map/ppermute | solution.py:67
  7.4 1.7 shard_map.175
  11.1 7.8 %collective-permute-done.4.refs_5_ = bf16[32,512]{1,0:T(8,128)(2,1)S(1)} collective-permute-done((bf16[32,512]{1,0:T(8,128)(2,1)}, bf16[32,512]{1,0:T(8,128)(2,1)S(1)}, u32[]{:S(2)}, u32[]{:S(2)}) %collective-permute-start.4) | collective-permute-done | bytes 32800 | tf_op jit(solution)/shard_map/ppermute | solution.py:67
  21.7 1.8 collective-permute-start.5
  23.5 3.7 %collective-permute-start.6 = (bf16[64,4096]{1,0:T(8,128)(2,1)S(1)}, bf16[64,4096]{1,0:T(8,128)(2,1)S(1)}, u32[]{:S(2)}, u32[]{:S(2)}) collective-permute-start(bf16[64,4096]{1,0:T(8,128)(2,1)S(1)} %get-tuple-element.51.refs_2_), channel_id=1, source_target_pairs={{0,24},{1,3},{2,26},{3,1},{4,28},{5,7},{6,30},{7,5},{8,16},{9,11},... | collective-permute-start | bytes 1572872 | tf_op jit(solution)/shard_map/ppermute | solution.py:67
  27.3 11.0 %collective-permute-done.7.refs_5_ = bf16[64,512]{1,0:T(8,128)(2,1)S(1)} collective-permute-done((bf16[64,512]{1,0:T(8,128)(2,1)S(1)}, bf16[64,512]{1,0:T(8,128)(2,1)S(1)}, u32[]{:S(2)}, u32[]{:S(2)}) %collective-permute-start.7) | collective-permute-done | bytes 65568 | tf_op jit(solution)/shard_map/ppermute | solution.py:67
  38.4 2.3 %collective-permute-start.8 = (bf16[1024,512]{1,0:T(8,128)(2,1)S(1)}, bf16[1024,512]{1,0:T(8,128)(2,1)S(1)}, u32[]{:S(2)}, u32[]{:S(2)}) collective-permute-start(bf16[1024,512]{1,0:T(8,128)(2,1)S(1)} %get-tuple-element.53.refs_0_), channel_id=1, source_target_pairs={{0,8},{1,25},{2,10},{3,27},{4,12},{5,29},{6,14},{7,31},{8,0},{9,17... | collective-permute-start | bytes 3145736 | tf_op jit(solution)/shard_map/ppermute | solution.py:67
  42.7 5.1 %shard_map.173 = (bf16[192,4096]{1,0:T(8,128)(2,1)}, bf16[192,4096]{1,0:T(8,128)(2,1)}) custom-call(s32[17]{0:T(128)} %pad_add_fusion.info, bf16[192,8192]{1,0:T(8,128)(2,1)} %x_ref.1), custom_call_target="tpu_custom_call" | custom-call | bytes 6291456 | tf_op jit(solution)/shard_map/pallas_call | solution.py:207
  47.9 9.0 %collective-permute-done.10.refs_5_ = bf16[128,512]{1,0:T(8,128)(2,1)S(1)} collective-permute-done((bf16[128,512]{1,0:T(8,128)(2,1)S(1)}, bf16[128,512]{1,0:T(8,128)(2,1)S(1)}, u32[]{:S(2)}, u32[]{:S(2)}) %collective-permute-start.10) | collective-permute-done | bytes 131104 | tf_op jit(solution)/shard_map/ppermute | solution.py:67
  57.5 5.8 %collective-permute-done.8.refs_1_ = bf16[1024,512]{1,0:T(8,128)(2,1)S(1)} collective-permute-done((bf16[1024,512]{1,0:T(8,128)(2,1)S(1)}, bf16[1024,512]{1,0:T(8,128)(2,1)S(1)}, u32[]{:S(2)}, u32[]{:S(2)}) %collective-permute-start.8) | collective-permute-done | bytes 1048608 | tf_op jit(solution)/shard_map/ppermute | solution.py:67
  64.3 3.5 %shard_map.178 = (bf16[2048,512]{1,0:T(8,128)(2,1)}, bf16[256,4096]{1,0:T(8,128)(2,1)}, bf16[256,512]{1,0:T(8,128)(2,1)S(1)}) custom-call(bf16[1024,512]{1,0:T(8,128)(2,1)S(1)} %get-tuple-element.53.refs_0_, bf16[1024,512]{1,0:T(8,128)(2,1)S(1)} %collective-permute-done.8.refs_1_, bf16[128,4096]{1,0:T(8,128)(2,1)S(1)} %get-tuple-element.54.refs_2_, ...), custom_call_target="tpu_custom_call" | custom-call | bytes 8912896 | tf_op jit(solution)/shard_map/pallas_call | solution.py:89
  69.2 2.5 %collective-permute-start.12 = (bf16[2048,512]{1,0:T(8,128)(2,1)}, bf16[2048,512]{1,0:T(8,128)(2,1)}, u32[]{:S(2)}, u32[]{:S(2)}) collective-permute-start(bf16[2048,512]{1,0:T(8,128)(2,1)} %get-tuple-element.57.refs_8_), channel_id=1, source_target_pairs={{0,24},{1,3},{2,26},{3,1},{4,28},{5,7},{6,30},{7,5},{8,16},{9,11},... | collective-permute-start | bytes 6291464 | tf_op jit(solution)/shard_map/ppermute | solution.py:67
  78.0 4.0 %shard_map.180.add_ref = f32[384,128]{1,0:T(8,128)S(1)} custom-call(bf16[192,4096]{1,0:T(8,128)(2,1)S(1)} %copy-done.1, bf16[192,4096]{1,0:T(8,128)(2,1)} %collective-permute-done.refs_2_.refs_3_.y_ref, bf16[256,4096]{1,0:T(8,128)(2,1)S(1)} %copy-done.3, s32[1,256]{1,0:T(1,128)S(1)} %get-tuple-element.95.owner_ref, ...), custom_call_target="tpu_custom_call" | custom-call | flops 805306368 | bytes 5242880 | tf_op jit(solution)/shard_map/pallas_call | solution.py:294
  82.7 14.1 %collective-permute-done.14 = bf16[256,512]{1,0:T(8,128)(2,1)S(1)} collective-permute-done((bf16[256,512]{1,0:T(8,128)(2,1)S(1)}, bf16[256,512]{1,0:T(8,128)(2,1)S(1)}, u32[]{:S(2)}, u32[]{:S(2)}) %collective-permute-start.14) | collective-permute-done | bytes 262176 | tf_op jit(solution)/shard_map/ppermute | solution.py:67
  97.5 2.4 %gather_fusion = bf16[16,32,512]{2,1,0:T(8,128)(2,1)} fusion(bf16[16,32,512]{2,1,0:T(8,128)(2,1)} %bitcast.4, s32[1024]{0:T(1024)S(1)} %pad_clamp_fusion), kind=kCustom, calls=%fused_computation | custom fusion | bytes 1048640 | tf_op jit(solution)/shard_map/gather | solution.py:489
  101.6 4.6 %shard_map.181 = f32[384,128]{1,0:T(8,128)S(1)} custom-call(bf16[192,4096]{1,0:T(8,128)(2,1)S(1)} %copy-done.2, bf16[192,4096]{1,0:T(8,128)(2,1)} %collective-permute-done.refs_2_.refs_3_.y_ref, bf16[256,4096]{1,0:T(8,128)(2,1)S(1)} %collective-permute-done.11.refs_6_.refs_7_.a_ref.refs_3_, s32[1,256]{1,0:T(1,128)S(1)} %get-tuple-element.96.owner_ref, ...), custom_call_target="tpu_custom_call" | custom-call | flops 805306368 | bytes 5242880 | tf_op jit(solution)/shard_map/pallas_call | solution.py:294
  106.2 15.7 %collective-permute-start.16 = (f32[384,128]{1,0:T(8,128)S(1)}, f32[384,128]{1,0:T(8,128)S(1)}, u32[]{:S(2)}, u32[]{:S(2)}) collective-permute-start(f32[384,128]{1,0:T(8,128)S(1)} %shard_map.181), channel_id=1, source_target_pairs={{0,1},{1,0},{2,3},{3,2},{4,5},{5,4},{6,7},{7,6},{8,9},{9,8},{10,11... | collective-permute-start | bytes 589832 | tf_op jit(solution)/shard_map/ppermute | solution.py:60
  122.4 7.1 %shard_map.183 = (bf16[256,2048]{1,0:T(8,128)(2,1)S(1)}, bf16[256,2048]{1,0:T(8,128)(2,1)S(1)}, bf16[256,2048]{1,0:T(8,128)(2,1)S(1)}, bf16[256,2048]{1,0:T(8,128)(2,1)S(1)}) custom-call(bf16[512,384]{1,0:T(8,128)(2,1)S(1)} %fusion.4.low_ref, bf16[512,384]{1,0:T(8,128)(2,1)S(1)} %fusion.5.low_two_ref, ...), custom_call_target="tpu_custom_call" | custom-call | flops 1610612736 | bytes 7340032 | tf_op jit(solution)/shard_map/pallas_call | solution.py:251
  131.4 4.9 %collective-permute-start.18 = (bf16[256,2048]{1,0:T(8,128)(2,1)}, bf16[256,2048]{1,0:T(8,128)(2,1)S(1)}, u32[]{:S(2)}, u32[]{:S(2)}) collective-permute-start(bf16[256,2048]{1,0:T(8,128)(2,1)} %get-tuple-element.65), channel_id=1, source_target_pairs={{0,4},{1,9},{2,6},{3,11},{4,0},{5,13},{6,2},{7,15},{8,12},{9,1},{1... | collective-permute-start | bytes 3145736 | tf_op jit(solution)/shard_map/ppermute | solution.py:67
  136.3 5.2 %collective-permute-start.19 = (bf16[256,2048]{1,0:T(8,128)(2,1)}, bf16[256,2048]{1,0:T(8,128)(2,1)S(1)}, u32[]{:S(2)}, u32[]{:S(2)}) collective-permute-start(bf16[256,2048]{1,0:T(8,128)(2,1)} %get-tuple-element.67), channel_id=1, source_target_pairs={{0,24},{1,3},{2,26},{3,1},{4,28},{5,7},{6,30},{7,5},{8,16},{9,11},... | collective-permute-start | bytes 3145736 | tf_op jit(solution)/shard_map/ppermute | solution.py:67
  142.3 9.8 %collective-permute-done.26 = f32[256,256]{1,0:T(8,128)S(1)} collective-permute-done((f32[256,256]{1,0:T(8,128)S(1)}, f32[256,256]{1,0:T(8,128)S(1)}, u32[]{:S(2)}, u32[]{:S(2)}) %collective-permute-start.26) | collective-permute-done | bytes 262176 | tf_op jit(solution)/shard_map/ppermute | solution.py:67
  153.7 11.3 %collective-permute-done.19.refs_3_ = bf16[256,2048]{1,0:T(8,128)(2,1)S(1)} collective-permute-done((bf16[256,2048]{1,0:T(8,128)(2,1)}, bf16[256,2048]{1,0:T(8,128)(2,1)S(1)}, u32[]{:S(2)}, u32[]{:S(2)}) %collective-permute-start.19) | collective-permute-done | bytes 1048608 | tf_op jit(solution)/shard_map/ppermute | solution.py:67
  166.0 1.7 shard_map.185
  169.4 3.0 %collective-permute-start.28 = (f32[64,256]{1,0:T(8,128)S(1)}, f32[64,256]{1,0:T(8,128)S(1)}, u32[]{:S(2)}, u32[]{:S(2)}) collective-permute-start(f32[64,256]{1,0:T(8,128)S(1)} %get-tuple-element.92), channel_id=1, source_target_pairs={{0,24},{1,3},{2,26},{3,1},{4,28},{5,7},{6,30},{7,5},{8,16},{9,11},... | collective-permute-start | bytes 196616 | tf_op jit(solution)/shard_map/ppermute | solution.py:67
  173.8 11.4 %collective-permute-done.28 = f32[64,256]{1,0:T(8,128)S(1)} collective-permute-done((f32[64,256]{1,0:T(8,128)S(1)}, f32[64,256]{1,0:T(8,128)S(1)}, u32[]{:S(2)}, u32[]{:S(2)}) %collective-permute-start.28) | collective-permute-done | bytes 65568 | tf_op jit(solution)/shard_map/ppermute | solution.py:67
  186.1 10.8 %shard_map.179 = (f32[384,512]{1,0:T(8,128)S(1)}, bf16[192,4096]{1,0:T(8,128)(2,1)S(1)}, bf16[192,4096]{1,0:T(8,128)(2,1)S(1)}) custom-call(s32[17]{0:T(128)S(1)} %copy-done.15, bf16[192,4096]{1,0:T(8,128)(2,1)} %get-tuple-element.44.refs_0_.refs_1_.x_ref, bf16[192,4096]{1,0:T(8,128)(2,1)} %get-tuple-element.44.refs_0_.refs_1_.x_ref, ...), custom_call_target="tpu_custom_call" | custom-call | flops 4831838208 | bytes 14680064 | tf_op jit(solution)/shard_map/pallas_call | solution.py:344
  198.8 2.1 collective-permute-start.24
  200.8 1.9 collective-permute-done.25
  205.6 2.0 add_convert_fusion
  208.7 5.0 %shard_map.182 = bf16[192,8192]{1,0:T(8,128)(2,1)} custom-call(s32[17]{0:T(128)} %pad_add_fusion.info, bf16[192,4096]{1,0:T(8,128)(2,1)} %copy-done.5, bf16[192,4096]{1,0:T(8,128)(2,1)} %copy-done.18), custom_call_target="tpu_custom_call" | custom-call | bytes 6291456 | tf_op jit(solution)/shard_map/pallas_call | solution.py:387
  213.8 1.9 shard_map.188
  (135 shorter events, 37.1 us)
Async XLA Ops:
  3.8 2.9 %collective-permute-start.2 = (bf16[16,4608]{1,0:T(8,128)(2,1)}, bf16[16,4608]{1,0:T(8,128)(2,1)S(1)}, u32[]{:S(2)}, u32[]{:S(2)}) collective-permute-start(bf16[16,4608]{1,0:T(8,128)(2,1)} %get-tuple-element.47), channel_id=1, source_target_pairs={{0,1},{1,0},{2,3},{3,2},{4,5},{5,4},{6,7},{7,6},{8,9},{9,8},{10,11... | collective-permute-start | bytes 442376 | tf_op jit(solution)/shard_map/ppermute | solution.py:60
  4.2 14.7 %collective-permute-start.1 = (bf16[256,512]{1,0:T(8,128)(2,1)}, bf16[256,512]{1,0:T(8,128)(2,1)S(1)}, u32[]{:S(2)}, u32[]{:S(2)}) collective-permute-start(bf16[256,512]{1,0:T(8,128)(2,1)} %refs_0_.1), channel_id=1, source_target_pairs={{0,2},{1,5},{2,0},{3,7},{4,6},{5,1},{6,4},{7,3},{8,10},{9,13},{10,... | collective-permute-start | bytes 786440 | tf_op jit(solution)/shard_map/ppermute | solution.py:67
  9.1 9.9 %collective-permute-start.3 = (bf16[32,4096]{1,0:T(8,128)(2,1)}, bf16[32,4096]{1,0:T(8,128)(2,1)S(1)}, u32[]{:S(2)}, u32[]{:S(2)}) collective-permute-start(bf16[32,4096]{1,0:T(8,128)(2,1)} %get-tuple-element.48.refs_2_), channel_id=1, source_target_pairs={{0,8},{1,25},{2,10},{3,27},{4,12},{5,29},{6,14},{7,31},{8,0},{9,17... | collective-permute-start | bytes 786440 | tf_op jit(solution)/shard_map/ppermute | solution.py:67
  10.7 8.2 %collective-permute-start.4 = (bf16[32,512]{1,0:T(8,128)(2,1)}, bf16[32,512]{1,0:T(8,128)(2,1)S(1)}, u32[]{:S(2)}, u32[]{:S(2)}) collective-permute-start(bf16[32,512]{1,0:T(8,128)(2,1)} %get-tuple-element.49.refs_4_), channel_id=1, source_target_pairs={{0,8},{1,25},{2,10},{3,27},{4,12},{5,29},{6,14},{7,31},{8,0},{9,17... | collective-permute-start | bytes 98312 | tf_op jit(solution)/shard_map/ppermute | solution.py:67
  21.7 16.6 %collective-permute-start.5 = (bf16[512,512]{1,0:T(8,128)(2,1)S(1)}, bf16[512,512]{1,0:T(8,128)(2,1)S(1)}, u32[]{:S(2)}, u32[]{:S(2)}) collective-permute-start(bf16[512,512]{1,0:T(8,128)(2,1)S(1)} %get-tuple-element.50.refs_0_), channel_id=1, source_target_pairs={{0,4},{1,9},{2,6},{3,11},{4,0},{5,13},{6,2},{7,15},{8,12},{9,1},{1... | collective-permute-start | bytes 1572872 | tf_op jit(solution)/shard_map/ppermute | solution.py:67
  23.5 14.8 %collective-permute-start.6 = (bf16[64,4096]{1,0:T(8,128)(2,1)S(1)}, bf16[64,4096]{1,0:T(8,128)(2,1)S(1)}, u32[]{:S(2)}, u32[]{:S(2)}) collective-permute-start(bf16[64,4096]{1,0:T(8,128)(2,1)S(1)} %get-tuple-element.51.refs_2_), channel_id=1, source_target_pairs={{0,24},{1,3},{2,26},{3,1},{4,28},{5,7},{6,30},{7,5},{8,16},{9,11},... | collective-permute-start | bytes 1572872 | tf_op jit(solution)/shard_map/ppermute | solution.py:67
  27.2 11.1 %collective-permute-start.7 = (bf16[64,512]{1,0:T(8,128)(2,1)S(1)}, bf16[64,512]{1,0:T(8,128)(2,1)S(1)}, u32[]{:S(2)}, u32[]{:S(2)}) collective-permute-start(bf16[64,512]{1,0:T(8,128)(2,1)S(1)} %get-tuple-element.52.refs_4_), channel_id=1, source_target_pairs={{0,24},{1,3},{2,26},{3,1},{4,28},{5,7},{6,30},{7,5},{8,16},{9,11},... | collective-permute-start | bytes 196616 | tf_op jit(solution)/shard_map/ppermute | solution.py:67
  38.4 24.9 %collective-permute-start.8 = (bf16[1024,512]{1,0:T(8,128)(2,1)S(1)}, bf16[1024,512]{1,0:T(8,128)(2,1)S(1)}, u32[]{:S(2)}, u32[]{:S(2)}) collective-permute-start(bf16[1024,512]{1,0:T(8,128)(2,1)S(1)} %get-tuple-element.53.refs_0_), channel_id=1, source_target_pairs={{0,8},{1,25},{2,10},{3,27},{4,12},{5,29},{6,14},{7,31},{8,0},{9,17... | collective-permute-start | bytes 3145736 | tf_op jit(solution)/shard_map/ppermute | solution.py:67
  40.7 22.7 %collective-permute-start.9 = (bf16[128,4096]{1,0:T(8,128)(2,1)S(1)}, bf16[128,4096]{1,0:T(8,128)(2,1)}, u32[]{:S(2)}, u32[]{:S(2)}) collective-permute-start(bf16[128,4096]{1,0:T(8,128)(2,1)S(1)} %get-tuple-element.54.refs_2_), channel_id=1, source_target_pairs={{0,2},{1,5},{2,0},{3,7},{4,6},{5,1},{6,4},{7,3},{8,10},{9,13},{10,... | collective-permute-start | bytes 3145736 | tf_op jit(solution)/shard_map/ppermute | solution.py:67
  42.2 14.7 %collective-permute-start.10 = (bf16[128,512]{1,0:T(8,128)(2,1)S(1)}, bf16[128,512]{1,0:T(8,128)(2,1)S(1)}, u32[]{:S(2)}, u32[]{:S(2)}) collective-permute-start(bf16[128,512]{1,0:T(8,128)(2,1)S(1)} %get-tuple-element.55.refs_4_), channel_id=1, source_target_pairs={{0,2},{1,5},{2,0},{3,7},{4,6},{5,1},{6,4},{7,3},{8,10},{9,13},{10,... | collective-permute-start | bytes 393224 | tf_op jit(solution)/shard_map/ppermute | solution.py:67
  42.7 29.4 %copy-start.24 = (s32[16]{0:T(128)S(1)}, s32[16]{0:T(128)}, u32[]{:S(2)}) copy-start(s32[16]{0:T(128)} %constant.65) | copy-start | bytes 196
  47.8 28.5 %collective-permute-start = (bf16[192,4096]{1,0:T(8,128)(2,1)}, bf16[192,4096]{1,0:T(8,128)(2,1)}, u32[]{:S(2)}, u32[]{:S(2)}) collective-permute-start(bf16[192,4096]{1,0:T(8,128)(2,1)} %get-tuple-element.45), channel_id=1, source_target_pairs={{0,1},{1,0},{2,3},{3,2},{4,5},{5,4},{6,7},{7,6},{8,9},{9,8},{10,11... | collective-permute-start | bytes 4718600 | tf_op jit(solution)/shard_map/ppermute | solution.py:60
  67.7 33.8 %collective-permute-start.11 = (bf16[256,4096]{1,0:T(8,128)(2,1)}, bf16[256,4096]{1,0:T(8,128)(2,1)S(1)}, u32[]{:S(2)}, u32[]{:S(2)}) collective-permute-start(bf16[256,4096]{1,0:T(8,128)(2,1)} %get-tuple-element.56.refs_4_.refs_5_.a_ref), channel_id=1, source_target_pairs={{0,4},{1,9},{2,6},{3,11},{4,0},{5,13},{6,2},{7,15},{8,12},{9,1},{1... | collective-permute-start | bytes 6291464 | tf_op jit(solution)/shard_map/ppermute | solution.py:67
  69.2 62.2 %collective-permute-start.12 = (bf16[2048,512]{1,0:T(8,128)(2,1)}, bf16[2048,512]{1,0:T(8,128)(2,1)}, u32[]{:S(2)}, u32[]{:S(2)}) collective-permute-start(bf16[2048,512]{1,0:T(8,128)(2,1)} %get-tuple-element.57.refs_8_), channel_id=1, source_target_pairs={{0,24},{1,3},{2,26},{3,1},{4,28},{5,7},{6,30},{7,5},{8,16},{9,11},... | collective-permute-start | bytes 6291464 | tf_op jit(solution)/shard_map/ppermute | solution.py:67
  72.0 1.6 collective-permute-start.13
  74.5 22.3 %collective-permute-start.14 = (bf16[256,512]{1,0:T(8,128)(2,1)S(1)}, bf16[256,512]{1,0:T(8,128)(2,1)S(1)}, u32[]{:S(2)}, u32[]{:S(2)}) collective-permute-start(bf16[256,512]{1,0:T(8,128)(2,1)S(1)} %get-tuple-element.58), channel_id=1, source_target_pairs={{0,4},{1,9},{2,6},{3,11},{4,0},{5,13},{6,2},{7,15},{8,12},{9,1},{1... | collective-permute-start | bytes 786440 | tf_op jit(solution)/shard_map/ppermute | solution.py:67
  106.2 35.3 %collective-permute-start.16 = (f32[384,128]{1,0:T(8,128)S(1)}, f32[384,128]{1,0:T(8,128)S(1)}, u32[]{:S(2)}, u32[]{:S(2)}) collective-permute-start(f32[384,128]{1,0:T(8,128)S(1)} %shard_map.181), channel_id=1, source_target_pairs={{0,1},{1,0},{2,3},{3,2},{4,5},{5,4},{6,7},{7,6},{8,9},{9,8},{10,11... | collective-permute-start | bytes 589832 | tf_op jit(solution)/shard_map/ppermute | solution.py:60
  131.4 22.3 %collective-permute-start.18 = (bf16[256,2048]{1,0:T(8,128)(2,1)}, bf16[256,2048]{1,0:T(8,128)(2,1)S(1)}, u32[]{:S(2)}, u32[]{:S(2)}) collective-permute-start(bf16[256,2048]{1,0:T(8,128)(2,1)} %get-tuple-element.65), channel_id=1, source_target_pairs={{0,4},{1,9},{2,6},{3,11},{4,0},{5,13},{6,2},{7,15},{8,12},{9,1},{1... | collective-permute-start | bytes 3145736 | tf_op jit(solution)/shard_map/ppermute | solution.py:67
  136.3 28.8 %collective-permute-start.19 = (bf16[256,2048]{1,0:T(8,128)(2,1)}, bf16[256,2048]{1,0:T(8,128)(2,1)S(1)}, u32[]{:S(2)}, u32[]{:S(2)}) collective-permute-start(bf16[256,2048]{1,0:T(8,128)(2,1)} %get-tuple-element.67), channel_id=1, source_target_pairs={{0,24},{1,3},{2,26},{3,1},{4,28},{5,7},{6,30},{7,5},{8,16},{9,11},... | collective-permute-start | bytes 3145736 | tf_op jit(solution)/shard_map/ppermute | solution.py:67
  142.2 9.9 %collective-permute-start.26 = (f32[256,256]{1,0:T(8,128)S(1)}, f32[256,256]{1,0:T(8,128)S(1)}, u32[]{:S(2)}, u32[]{:S(2)}) collective-permute-start(f32[256,256]{1,0:T(8,128)S(1)} %slice.120), channel_id=1, source_target_pairs={{0,4},{1,9},{2,6},{3,11},{4,0},{5,13},{6,2},{7,15},{8,12},{9,1},{1... | collective-permute-start | bytes 786440 | tf_op jit(solution)/shard_map/ppermute | solution.py:67
  152.1 17.2 %collective-permute-start.27 = (f32[128,256]{1,0:T(8,128)S(1)}, f32[128,256]{1,0:T(8,128)S(1)}, u32[]{:S(2)}, u32[]{:S(2)}) collective-permute-start(f32[128,256]{1,0:T(8,128)S(1)} %get-tuple-element.88), channel_id=1, source_target_pairs={{0,2},{1,5},{2,0},{3,7},{4,6},{5,1},{6,4},{7,3},{8,10},{9,13},{10,... | collective-permute-start | bytes 393224 | tf_op jit(solution)/shard_map/ppermute | solution.py:67
  167.7 17.5 %collective-permute-start.20 = (bf16[128,2048]{1,0:T(8,128)(2,1)S(1)}, bf16[128,2048]{1,0:T(8,128)(2,1)S(1)}, u32[]{:S(2)}, u32[]{:S(2)}) collective-permute-start(bf16[128,2048]{1,0:T(8,128)(2,1)S(1)} %get-tuple-element.69), channel_id=1, source_target_pairs={{0,2},{1,5},{2,0},{3,7},{4,6},{5,1},{6,4},{7,3},{8,10},{9,13},{10,... | collective-permute-start | bytes 1572872 | tf_op jit(solution)/shard_map/ppermute | solution.py:67
  169.3 16.0 %collective-permute-start.21 = (bf16[128,2048]{1,0:T(8,128)(2,1)S(1)}, bf16[128,2048]{1,0:T(8,128)(2,1)S(1)}, u32[]{:S(2)}, u32[]{:S(2)}) collective-permute-start(bf16[128,2048]{1,0:T(8,128)(2,1)S(1)} %get-tuple-element.71), channel_id=1, source_target_pairs={{0,8},{1,25},{2,10},{3,27},{4,12},{5,29},{6,14},{7,31},{8,0},{9,17... | collective-permute-start | bytes 1572872 | tf_op jit(solution)/shard_map/ppermute | solution.py:67
  169.4 15.9 %collective-permute-start.28 = (f32[64,256]{1,0:T(8,128)S(1)}, f32[64,256]{1,0:T(8,128)S(1)}, u32[]{:S(2)}, u32[]{:S(2)}) collective-permute-start(f32[64,256]{1,0:T(8,128)S(1)} %get-tuple-element.92), channel_id=1, source_target_pairs={{0,24},{1,3},{2,26},{3,1},{4,28},{5,7},{6,30},{7,5},{8,16},{9,11},... | collective-permute-start | bytes 196616 | tf_op jit(solution)/shard_map/ppermute | solution.py:67
  185.3 13.5 %collective-permute-start.29 = (f32[32,256]{1,0:T(8,128)S(1)}, f32[32,256]{1,0:T(8,128)S(1)}, u32[]{:S(2)}, u32[]{:S(2)}) collective-permute-start(f32[32,256]{1,0:T(8,128)S(1)} %slice_add_fusion.4), channel_id=1, source_target_pairs={{0,8},{1,25},{2,10},{3,27},{4,12},{5,29},{6,14},{7,31},{8,0},{9,17... | collective-permute-start | bytes 98312 | tf_op jit(solution)/shard_map/ppermute | solution.py:67
  185.6 12.0 %collective-permute-start.22 = (bf16[64,2048]{1,0:T(8,128)(2,1)S(1)}, bf16[64,2048]{1,0:T(8,128)(2,1)S(1)}, u32[]{:S(2)}, u32[]{:S(2)}) collective-permute-start(bf16[64,2048]{1,0:T(8,128)(2,1)S(1)} %get-tuple-element.73), channel_id=1, source_target_pairs={{0,24},{1,3},{2,26},{3,1},{4,28},{5,7},{6,30},{7,5},{8,16},{9,11},... | collective-permute-start | bytes 786440 | tf_op jit(solution)/shard_map/ppermute | solution.py:67
  185.9 11.7 %collective-permute-start.23 = (bf16[64,2048]{1,0:T(8,128)(2,1)S(1)}, bf16[64,2048]{1,0:T(8,128)(2,1)S(1)}, u32[]{:S(2)}, u32[]{:S(2)}) collective-permute-start(bf16[64,2048]{1,0:T(8,128)(2,1)S(1)} %get-tuple-element.75), channel_id=1, source_target_pairs={{0,4},{1,9},{2,6},{3,11},{4,0},{5,13},{6,2},{7,15},{8,12},{9,1},{1... | collective-permute-start | bytes 786440 | tf_op jit(solution)/shard_map/ppermute | solution.py:67
  197.0 8.6 %collective-permute-start.15 = (f32[192,512]{1,0:T(8,128)S(1)}, f32[192,512]{1,0:T(8,128)S(1)}, u32[]{:S(2)}, u32[]{:S(2)}) collective-permute-start(f32[192,512]{1,0:T(8,128)S(1)} %slice.86), channel_id=1, source_target_pairs={{0,1},{1,0},{2,3},{3,2},{4,5},{5,4},{6,7},{7,6},{8,9},{9,8},{10,11... | collective-permute-start | bytes 1179656 | tf_op jit(solution)/shard_map/ppermute | solution.py:60
  197.0 10.5 %collective-permute-start.17 = (bf16[192,4096]{1,0:T(8,128)(2,1)S(1)}, bf16[192,4096]{1,0:T(8,128)(2,1)S(1)}, u32[]{:S(2)}, u32[]{:S(2)}) collective-permute-start(bf16[192,4096]{1,0:T(8,128)(2,1)S(1)} %get-tuple-element.61), channel_id=1, source_target_pairs={{0,1},{1,0},{2,3},{3,2},{4,5},{5,4},{6,7},{7,6},{8,9},{9,8},{10,11... | collective-permute-start | bytes 4718600 | tf_op jit(solution)/shard_map/ppermute | solution.py:60
  197.7 5.0 %collective-permute-start.25 = (bf16[32,2048]{1,0:T(8,128)(2,1)S(1)}, bf16[32,2048]{1,0:T(8,128)(2,1)S(1)}, u32[]{:S(2)}, u32[]{:S(2)}) collective-permute-start(bf16[32,2048]{1,0:T(8,128)(2,1)S(1)} %get-tuple-element.79), channel_id=1, source_target_pairs={{0,2},{1,5},{2,0},{3,7},{4,6},{5,1},{6,4},{7,3},{8,10},{9,13},{10,... | collective-permute-start | bytes 393224 | tf_op jit(solution)/shard_map/ppermute | solution.py:67
  198.8 5.0 %collective-permute-start.24 = (bf16[32,2048]{1,0:T(8,128)(2,1)S(1)}, bf16[32,2048]{1,0:T(8,128)(2,1)S(1)}, u32[]{:S(2)}, u32[]{:S(2)}) collective-permute-start(bf16[32,2048]{1,0:T(8,128)(2,1)S(1)} %get-tuple-element.77), channel_id=1, source_target_pairs={{0,8},{1,25},{2,10},{3,27},{4,12},{5,29},{6,14},{7,31},{8,0},{9,17... | collective-permute-start | bytes 393224 | tf_op jit(solution)/shard_map/ppermute | solution.py:67
  203.9 9.8 %collective-permute-start.30 = (f32[16,4352]{1,0:T(8,128)S(1)}, f32[16,4352]{1,0:T(8,128)S(1)}, u32[]{:S(2)}, u32[]{:S(2)}) collective-permute-start(f32[16,4352]{1,0:T(8,128)S(1)} %get-tuple-element.89), channel_id=1, source_target_pairs={{0,1},{1,0},{2,3},{3,2},{4,5},{5,4},{6,7},{7,6},{8,9},{9,8},{10,11... | collective-permute-start | bytes 835592 | tf_op jit(solution)/shard_map/ppermute | solution.py:60
  (24 other events, 140.5 us)

commit v3 on v1

v3 whole, which is shorter than its diff:
```python
import functools
import math

import jax
import jax.numpy as jnp
from jax import lax
from jax.experimental import pallas as pl
from jax.experimental.pallas import tpu as pltpu
from jax.sharding import PartitionSpec as P

adapter_scale = 0.25
beta_first = 0.9
beta_second = 0.95
adam_eps = 1e-08
learn_rate = 0.05
bias_first = 0.271
bias_second = 0.142625
contract_last = (((1,), (1,)), ((), ()))
contract_first = (((0,), (0,)), ((), ()))
f32 = jnp.float32
bf16 = jnp.bfloat16
vmem_bytes = 24 * 2**20


def dot(a, b, dims=(((1,), (0,)), ((), ()))):
    return lax.dot_general(a, b, dims, preferred_element_type=f32)


team = 4


class Plan:
    def __init__(self, devices):
        self.devices = devices
        self.teams = devices // team
        self.bits = self.teams.bit_length() - 1
        down = tuple(1 << i for i in reversed(range(self.bits)))
        self.orders = {"w": down, "d": down[-1:] + down[:-1]}

    def masks(self, stream):
        out = []
        for b in range(self.teams):
            m = 0
            for i, flip in enumerate(self.orders[stream]):
                if b >> i & 1:
                    m ^= flip
            out.append(m)
        return out

    def member(self, x, k):
        return lax.ppermute(x, "fsdp", [(i, i ^ k) for i in range(self.devices)])

    def step(self, x, stream, i):
        flip = self.orders[stream][i] * team
        return lax.ppermute(x, "fsdp", [(d, d ^ flip) for d in range(self.devices)])


def estimate(flops, bytes_accessed, transcendentals):
    return pl.CostEstimate(
        flops=flops // 1, bytes_accessed=bytes_accessed // 1, transcendentals=transcendentals
    )


def hbm(x):
    return pltpu.with_memory_space_constraint(x, pltpu.HBM)


whole_vmem = pl.BlockSpec(memory_space=pltpu.VMEM)
anywhere = pl.BlockSpec(memory_space=pl.ANY)


def params():
    return pltpu.CompilerParams(vmem_limit_bytes=vmem_bytes)


def join_kernel(count, late, *refs):
    refs = refs[: 2 * count] + refs[2 * count + late :]
    for i in range(count):
        own, got, out = refs[2 * i], refs[2 * i + 1], refs[2 * count + i]
        rows = own.shape[0]
        out[:rows] = own[...]
        out[rows:] = got[...]


def join(pairs, after=()):
    count = len(pairs)
    flat = [x for pair in pairs for x in pair]
    return pl.pallas_call(
        functools.partial(join_kernel, count, len(after)),
        in_specs=[whole_vmem] * (2 * count) + [anywhere] * len(after),
        out_specs=[whole_vmem] * count,
        out_shape=[jax.ShapeDtypeStruct((2 * x.shape[0], x.shape[1]), x.dtype) for x, _ in pairs],
        compiler_params=params(),
        cost_estimate=estimate(
            flops=0, bytes_accessed=4 * sum(x.size for x in flat), transcendentals=0
        ),
    )(*flat, *after)


def fold_kernel(count, late, *refs):
    refs = refs[: 2 * count] + refs[2 * count + late :]
    for i in range(count):
        keep, got = refs[2 * i], refs[2 * i + 1]
        kept, sent = refs[2 * count + 2 * i], refs[2 * count + 2 * i + 1]
        half = kept.shape[0]
        kept[...] = (keep[:half].astype(f32) + got[:half].astype(f32)).astype(kept.dtype)
        sent[...] = (keep[half:].astype(f32) + got[half:].astype(f32)).astype(sent.dtype)


def fold(pairs, after=()):
    count = len(pairs)
    flat = [x for pair in pairs for x in pair]
    shapes = [
        jax.ShapeDtypeStruct((x.shape[0] // 2, x.shape[1]), x.dtype) for x, _ in pairs for _ in "ks"
    ]
    out = pl.pallas_call(
        functools.partial(fold_kernel, count, len(after)),
        in_specs=[whole_vmem] * (2 * count) + [anywhere] * len(after),
        out_specs=[whole_vmem] * (2 * count),
        out_shape=shapes,
        compiler_params=params(),
        cost_estimate=estimate(
            flops=sum(x.size for x in flat),
            bytes_accessed=4 * sum(x.size for x in flat),
            transcendentals=0,
        ),
    )(*flat, *after)
    return [(out[2 * i], out[2 * i + 1]) for i in range(count)]


def tie_kernel(*refs):
    del refs


def tie(arrays, after):
    count = len(arrays)
    return pl.pallas_call(
        tie_kernel,
        in_specs=[anywhere] * (count + len(after)),
        out_specs=[anywhere] * count,
        out_shape=[jax.ShapeDtypeStruct(x.shape, x.dtype) for x in arrays],
        input_output_aliases={i: i for i in range(count)},
        cost_estimate=estimate(flops=0, bytes_accessed=0, transcendentals=0),
    )(*arrays, *after)


def members_of(info):
    j = info[0]
    return [j ^ k for k in range(team)]


def factor_kernel(width, wide, info, f_ref, *refs):
    quarter = wide // team
    for j, ref in zip(members_of(info), refs):
        for q in range(quarter // width):
            at = pl.multiple_of((team * q + j) * width, width)
            ref[:, q * width : (q + 1) * width] = f_ref[:, pl.ds(at, width)].astype(bf16)
        ref[:, quarter:] = f_ref[:, wide:].astype(bf16)


def split_factors(info, factors, width, wide):
    rank, total = factors.shape
    shape = jax.ShapeDtypeStruct((rank, wide // team + total - wide), bf16)
    return pl.pallas_call(
        functools.partial(factor_kernel, width, wide),
        in_specs=[pl.BlockSpec(memory_space=pltpu.SMEM), whole_vmem],
        out_specs=[whole_vmem] * team,
        out_shape=[shape] * team,
        cost_estimate=estimate(flops=0, bytes_accessed=1_000_000, transcendentals=0),
    )(info, factors)


def join_factors_kernel(quarter, *refs):
    up_ref, down_ref = refs[team:]
    rank = refs[0].shape[0]
    for k in range(team):
        down_ref[k * rank : (k + 1) * rank] = refs[k][:, :quarter]
        up_ref[k * rank : (k + 1) * rank] = refs[k][:, quarter:]


def join_factors(parts, quarter):
    rank, total = parts[0].shape
    return pl.pallas_call(
        functools.partial(join_factors_kernel, quarter),
        in_specs=[whole_vmem] * team,
        out_specs=[whole_vmem] * 2,
        out_shape=[
            jax.ShapeDtypeStruct((team * rank, total - quarter), bf16),
            jax.ShapeDtypeStruct((team * rank, quarter), bf16),
        ],
        cost_estimate=estimate(flops=0, bytes_accessed=16 * rank * total, transcendentals=0),
    )(*parts)


def deal_kernel(width, info, x_ref, t_ref, own_ref, *refs):
    quarter = own_ref.shape[1]
    for k, j in enumerate(members_of(info)):
        ref = refs[k - 1] if k else own_ref
        for q in range(quarter // width):
            at = pl.multiple_of((team * q + j) * width, width)
            ref[:, q * width : (q + 1) * width] = x_ref[:, pl.ds(at, width)]
        if k:
            ref[:, quarter:] = t_ref[...]


def deal(info, x, tail, width):
    rows, wide = x.shape
    step = rows // 6
    quarter = wide // team
    row = lambda n: pl.BlockSpec((step, n), lambda i, s: (i, 0))
    more = quarter + tail.shape[1]
    return pl.pallas_call(
        functools.partial(deal_kernel, width),
        grid_spec=pltpu.PrefetchScalarGridSpec(
            num_scalar_prefetch=1,
            grid=(6,),
            in_specs=[row(wide), row(tail.shape[1])],
            out_specs=[row(quarter)] + [row(more)] * (team - 1),
        ),
        out_shape=[jax.ShapeDtypeStruct((rows, quarter), bf16)]
        + [jax.ShapeDtypeStruct((rows, more), bf16)] * (team - 1),
        cost_estimate=estimate(flops=0, bytes_accessed=rows * wide * 4, transcendentals=0),
    )(info, x, tail)


def down_grad_kernel(half, scale, low_ref, low_two_ref, *refs):
    xs, (ka, sa, kb, sb) = refs[:team], refs[team:]
    q = pl.program_id(0)
    x = jnp.concatenate([ref[...] for ref in xs], axis=0)

    def one(low, keep, send):
        out = (scale * dot(low[...], x)).astype(bf16)
        cut = out.shape[0] // 2
        keep[...] = out[:cut]
        send[...] = out[cut:]

    @pl.when(q < half)
    def _():
        one(low_ref, ka, sa)

    @pl.when(q >= half)
    def _():
        one(low_two_ref, kb, sb)


def down_grads(low, low_two, xs, scale):
    rows, cols = xs[0].shape
    blocks = 4
    width = cols // blocks
    half = blocks // 2
    n = low.shape[0]
    whole = pl.BlockSpec(low.shape, lambda q: (0, 0))
    part = pl.BlockSpec((rows, width), lambda q: (0, q))
    first = pl.BlockSpec((n // 2, width), lambda q: (0, jnp.minimum(q, half - 1)))
    second = pl.BlockSpec((n // 2, width), lambda q: (0, jnp.maximum(q - half, 0)))
    out = pltpu.HBM((n // 2, cols // 2), bf16)
    return pl.pallas_call(
        functools.partial(down_grad_kernel, half, scale),
        grid=(blocks,),
        in_specs=[whole, whole] + [part] * team,
        out_specs=[first, first, second, second],
        out_shape=[out] * 4,
        compiler_params=params(),
        cost_estimate=estimate(
            flops=2 * team * rows * cols * n,
            bytes_accessed=2 * team * rows * cols + 2 * n * cols,
            transcendentals=0,
        ),
    )(low, low_two, *map(hbm, xs))


def project_kernel(rank, *refs):
    xs, (a_ref, owner_ref, target_ref, add_ref, o_ref, acc) = refs[:team], refs[team:]
    q = pl.program_id(0)

    @pl.when(q == 0)
    def _():
        acc[...] = jnp.zeros_like(acc)

    for k in range(team):
        acc[k] += dot(a_ref[...], xs[k][...], contract_last)

    @pl.when(q == pl.num_programs(0) - 1)
    def _():
        for k in range(team):
            kept = jnp.where(target_ref[k : k + 1] == owner_ref[...], acc[k], 0.0)
            at = slice(k * rank, (k + 1) * rank)
            out = add_ref[at]
            for i in range(kept.shape[0] // rank):
                out = out + kept[i * rank : (i + 1) * rank]
            o_ref[at] = out


def project(xs, down, owner, targets, add):
    rows, cols = xs[0].shape[0], down.shape[1]
    n = down.shape[0]
    width = cols // 4
    part = pl.BlockSpec((rows, width), lambda q: (0, q))
    still = lambda q: (0, 0)
    return pl.pallas_call(
        functools.partial(project_kernel, add.shape[0] // team),
        grid=(4,),
        in_specs=[part] * team
        + [
            pl.BlockSpec((n, width), lambda q: (0, q)),
            pl.BlockSpec((n, 1), still),
            pl.BlockSpec((team, rows), still),
            pl.BlockSpec(add.shape, still),
        ],
        out_specs=pl.BlockSpec(add.shape, still),
        out_shape=jax.ShapeDtypeStruct(add.shape, f32),
        scratch_shapes=[pltpu.VMEM((team, n, rows), f32)],
        compiler_params=params(),
        cost_estimate=estimate(
            flops=2 * team * rows * cols * n,
            bytes_accessed=2 * (team * rows + n) * cols,
            transcendentals=0,
        ),
    )(*map(hbm, (*xs, down, owner, targets, add)))


def lora_kernel(scale, *refs):
    parts, (owner_ref, target_ref, g_ref, up_ref, keep_ref, send_ref, v_ref) = refs[:team], refs[team:]
    rank = parts[0].shape[0] // team
    rows = parts[0].shape[1]
    count = owner_ref.shape[0]
    grad = None
    for m in range(team):
        total = None
        for k in range(team):
            one = parts[k][(m ^ k) * rank : ((m ^ k) + 1) * rank]
            total = one if total is None else total + one
        rounded = (scale * total).astype(bf16).astype(f32)
        many = jnp.concatenate([rounded] * (count // rank), axis=0)
        own = jnp.where(target_ref[m : m + 1] == owner_ref[...], many, 0.0).astype(bf16)
        more = dot(own, g_ref[m * rows : (m + 1) * rows])
        grad = more if grad is None else grad + more
        if m == 0:
            v_ref[...] = adapter_scale * dot(own, up_ref[...], contract_first)
    cut = count // 2
    keep_ref[...] = adapter_scale * grad[:cut]
    send_ref[...] = adapter_scale * grad[cut:]


def lora(parts, owner, targets, grads, up, scale):
    rows = parts[0].shape[1]
    half = jax.ShapeDtypeStruct((up.shape[0] // 2, grads.shape[1]), f32)
    return pl.pallas_call(
        functools.partial(lora_kernel, scale),
        in_specs=[whole_vmem] * (team + 4),
        out_specs=[whole_vmem] * 3,
        out_shape=[half, half, jax.ShapeDtypeStruct((rows, up.shape[1]), f32)],
        compiler_params=params(),
        cost_estimate=estimate(
            flops=2 * rows * up.size, bytes_accessed=2_000_000, transcendentals=0
        ),
    )(*parts, owner, targets, grads, up)


def frozen_kernel(half, width, scale, info, *refs):
    x0, x1, y0, y1, a0, a1, b0, b1, u_ref, w_ref, g_ref, low_ref, o_ref, t_ref, v_ref, acc = refs
    b = pl.program_id(0)

    @pl.when(b == 0)
    def _():
        acc[...] = jnp.zeros_like(acc)

    n = x0.shape[0]
    cut = a0.shape[0]
    acc[:n] += dot(x0[...], u_ref[...]) + dot(x1[...], w_ref[...])
    acc[n:] += dot(y0[...], u_ref[...]) + dot(y1[...], w_ref[...])
    for part, one, two, rows in ((0, a0, b0, u_ref), (half, a1, b1, w_ref)):
        lora = scale * (dot(low_ref[:, :cut], one[...]) + dot(low_ref[:, cut:], two[...]))
        out = dot(g_ref[...], rows[...], contract_last) + lora.astype(bf16).astype(f32)
        out = out.astype(bf16)
        at = pl.ds(pl.multiple_of(info[1 + part + b] * width, width), width)
        o_ref[:, at] = out[:n]
        t_ref[:, at] = out[n:]

    @pl.when(b == pl.num_programs(0) - 1)
    def _():
        quarter = o_ref.shape[1] - acc.shape[1]
        o_ref[:, quarter:] = acc[:n].astype(bf16)
        t_ref[:, quarter:] = acc[n:].astype(bf16)
        v_ref[...] = acc[:n]


def frozen(info, x, y, grads, low, downs, weights, width, scale, at):
    rows, kv = x.shape[0], grads.shape[1]
    n, cols = downs[0].shape
    half = cols // width // 2
    pair = lambda b, s: (at, 0)
    still = lambda b, s: (0, 0)
    early = lambda b, s: (0, s[1 + b])
    late = lambda b, s: (0, s[1 + half + b])
    out = pltpu.HBM((rows, cols + kv), bf16)
    return pl.pallas_call(
        functools.partial(frozen_kernel, half, width, scale),
        grid_spec=pltpu.PrefetchScalarGridSpec(
            num_scalar_prefetch=1,
            grid=(half,),
            in_specs=[pl.BlockSpec((rows, width), early), pl.BlockSpec((rows, width), late)] * 2
            + [pl.BlockSpec((n, width), early), pl.BlockSpec((n, width), late)] * 2
            + [pl.BlockSpec((width, kv), lambda b, s: (b, 0))] * 2
            + [pl.BlockSpec((2 * rows, kv), pair), pl.BlockSpec((2 * rows, 2 * n), pair)],
            out_specs=[pl.BlockSpec((rows, cols + kv), still)] * 2 + [pl.BlockSpec((rows, kv), still)],
            scratch_shapes=[pltpu.VMEM((2 * rows, kv), f32)],
        ),
        out_shape=[out, out, pltpu.HBM((rows, kv), f32)],
        compiler_params=params(),
        cost_estimate=estimate(
            flops=8 * rows * cols * (n + kv),
            bytes_accessed=(8 * rows + 4 * n + 2 * kv) * cols,
            transcendentals=0,
        ),
    )(info, *map(hbm, (x, x, y, y, downs[0], downs[0], downs[1], downs[1], *weights, grads, low)))


def merge_kernel(width, quarter, info, *refs):
    o_ref = refs[team]
    for j, ref in zip(members_of(info), refs):
        for q in range(quarter // width):
            at = pl.multiple_of((team * q + j) * width, width)
            o_ref[:, pl.ds(at, width)] = ref[:, q * width : (q + 1) * width]


def merge(info, parts, width, quarter):
    rows, cols = parts[0].shape
    step = rows // 6
    small = pl.BlockSpec((step, cols), lambda i, s: (i, 0))
    return pl.pallas_call(
        functools.partial(merge_kernel, width, quarter),
        grid_spec=pltpu.PrefetchScalarGridSpec(
            num_scalar_prefetch=1,
            grid=(6,),
            in_specs=[small] * team,
            out_specs=pl.BlockSpec((step, team * quarter), lambda i, s: (i, 0)),
        ),
        out_shape=jax.ShapeDtypeStruct((rows, team * quarter), bf16),
        cost_estimate=estimate(flops=0, bytes_accessed=16 * rows * cols, transcendentals=0),
    )(info, *map(hbm, parts))


def adam_kernel(width, wide, info, f_ref, m_ref, v_ref, *refs):
    grads, (nf_ref, nm_ref, nv_ref) = refs[:team], refs[team:]
    quarter = wide // team
    tail = (f_ref.shape[1] - wide) // team

    def update(at, g):
        first = beta_first * m_ref[:, at] + (1.0 - beta_first) * g
        second = beta_second * v_ref[:, at] + (1.0 - beta_second) * g * g
        step = first / bias_first / (jnp.sqrt(second / bias_second) + adam_eps)
        nf_ref[:, at] = f_ref[:, at] - learn_rate * step
        nm_ref[:, at] = first
        nv_ref[:, at] = second

    for j, ref in zip(members_of(info), grads):
        for q in range(quarter // width):
            at = pl.multiple_of((team * q + j) * width, width)
            update(pl.ds(at, width), ref[:, q * width : (q + 1) * width].astype(f32))
        update(pl.ds(pl.multiple_of(wide + j * tail, tail), tail), ref[:, quarter:].astype(f32))


def adam(info, factors, first, second, grads, width, wide):
    shape = jax.ShapeDtypeStruct(factors.shape, f32)
    return pl.pallas_call(
        functools.partial(adam_kernel, width, wide),
        in_specs=[pl.BlockSpec(memory_space=pltpu.SMEM)] + [whole_vmem] * (3 + team),
        out_specs=[whole_vmem] * 3,
        out_shape=[shape] * 3,
        compiler_params=params(),
        cost_estimate=estimate(
            flops=20 * factors.size, bytes_accessed=32 * factors.size, transcendentals=0
        ),
    )(info, factors, first, second, *grads)


def local(
    tokens, out_grad, base_weight, adapter_ids, adapter_home, factors, first_moment, second_moment
):
    tok_count, wide = tokens.shape
    value_width = out_grad.shape[1]
    rank = factors.shape[1]
    width = base_weight.shape[0]
    plan = Plan(lax.axis_size("fsdp"))
    bits = plan.bits
    quarter = wide // team
    input_scale = 1.0 / math.sqrt(wide)
    me = lax.axis_index("fsdp").astype(jnp.int32)
    group, member = me // team, me % team
    mask_d = jnp.array(plan.masks("d"), jnp.int32)
    mask_w = jnp.array(plan.masks("w"), jnp.int32)
    info = jnp.concatenate([member[None], group ^ mask_w])

    weight = base_weight
    got_weight = plan.step(weight, "w", 0)
    parts = split_factors(info, factors[0], width, wide)
    got_parts = [plan.member(parts[k], k) for k in range(1, team)]

    columns = jnp.arange(plan.devices, dtype=jnp.int32)
    adapter_hot = (adapter_ids[:, None] == columns[None, :]).astype(jnp.int32)
    target = jnp.sum(adapter_hot * adapter_home[None, :], axis=1)
    tail = jnp.concatenate(
        [out_grad, jnp.broadcast_to(target[:, None], (tok_count, 128)).astype(bf16)], axis=1
    )
    dealt = deal(info, tokens, tail, width)
    got = [plan.member(dealt[k], k) for k in range(1, team)]
    xs = [dealt[0]] + got
    tails = jnp.concatenate([tail] + [x[:, quarter:] for x in got], axis=0)
    grads = tails[:, :value_width]
    targets = tails[:, value_width].astype(jnp.int32)
    target_rows = targets.reshape(team, tok_count)

    up, down = join_factors([parts[0]] + got_parts, quarter)
    (weight,) = join(((weight, got_weight),))
    up, down = join(((up, plan.step(up, "d", 0)), (down, plan.step(down, "d", 0))), (weight,))
    for i in range(1, bits - 1):
        (up,) = join(((up, plan.step(up, "d", i)),))
    (up_all,) = join(((up, plan.step(up, "d", bits - 1)),))
    for i in range(1, bits - 1):
        (weight,) = join(((weight, plan.step(weight, "w", i)),))
        (down,) = join(((down, plan.step(down, "d", i)),), (weight,))
    weights = (weight, plan.step(weight, "w", bits - 1))
    downs = (down, plan.step(down, "d", bits - 1))

    within = jnp.arange(team * rank, dtype=jnp.int32) // rank

    def owner_of(mask):
        return (team * (group ^ mask)[:, None] + (member ^ within)[None, :]).reshape(-1)

    owner = owner_of(mask_d)
    owner_two = owner_of(mask_w)
    places = jnp.array([plan.masks("d").index(m) for m in plan.masks("w")], jnp.int32)
    up_two = up_all.reshape(plan.teams, team * rank, value_width)[places].reshape(up_all.shape)

    def low_of(up, owner):
        out = adapter_scale * dot(up, grads, contract_last)
        return jnp.where(owner[:, None] == targets[None, :], out, 0.0).astype(bf16)

    low = adapter_scale * dot(grads, up_all, contract_last)
    low = jnp.where(targets[:, None] == owner[None, :], low, 0.0).astype(bf16)
    keep_a, send_a, keep_b, send_b = down_grads(
        low_of(up_all, owner), low_of(up_two, owner_two), xs, input_scale
    )
    n = down.shape[0]
    nothing = jnp.zeros((team * rank, tok_count), f32)
    part = project(xs, downs[0], owner[:n, None], target_rows, nothing)

    (info_far,) = tie((info,), (keep_a, part))
    send_a, send_b = tie((send_a, send_b), (weights[1], downs[1]))
    far = frozen(info_far, xs[2], xs[3], grads, low, downs, weights, width, input_scale, 1)
    (part,) = tie((part,), (far[2],))
    from_far = [plan.member(far[0], 2), plan.member(far[1], 3)]
    part = project(xs, downs[1], owner[n:, None], target_rows, part)
    near = frozen(info_far, xs[0], xs[1], grads, low, downs, weights, width, input_scale, 0)
    done = [near[0], plan.member(near[1], 1)] + from_far

    value_part = value_width // team
    part_grads = lax.dynamic_slice_in_dim(grads, member * value_part, value_part, 1)
    keep_up, send_up, own_values = lora(
        [part] + [plan.member(part, k) for k in range(1, team)],
        owner[:, None],
        target_rows,
        part_grads,
        up_all,
        input_scale,
    )
    got_up = plan.step(send_up, "d", bits - 1)
    first_up = got_up
    lora_up = keep_up
    for i in reversed(range(bits)):
        if i < bits - 1:
            got_up = plan.step(send_up, "d", i)
        if i > 0:
            ((keep_up, send_up),) = fold(((keep_up, got_up),))
    sum_up = keep_up + got_up

    for i in reversed(range(bits)):
        got_a = plan.step(send_a, "d", i)
        got_b = plan.step(send_b, "w", i)
        if i > 0:
            (keep_a, send_a), (keep_b, send_b) = fold(
                ((keep_a, got_a), (keep_b, got_b)), (first_up,) if i == bits - 1 else ()
            )
    sum_a = keep_a.astype(f32) + got_a.astype(f32)
    sum_b = keep_b.astype(f32) + got_b.astype(f32)

    sums = jnp.concatenate([sum_a, sum_b, sum_up], axis=1)
    mine = [sums[:rank]]
    for k in range(1, team):
        mine.append(plan.member(sums[k * rank : (k + 1) * rank].astype(bf16), k))
    new_factors, new_first, new_second = adam(
        info, factors[0], first_moment[0], second_moment[0], mine, width, wide
    )

    values = near[2]
    for x in done[1:]:
        values = values + x[:, quarter:].astype(f32)
    value_output = (values + own_values.astype(bf16).astype(f32)).astype(bf16)
    input_gradient = merge(info, done, width, quarter)
    return (value_output, input_gradient, new_factors[None], new_first[None], new_second[None])


def solution(mesh):
    placed = (
        P(("groups", "fsdp"), None),
        P(("groups", "fsdp"), None),
        P("fsdp", None),
        P(("groups", "fsdp")),
        P("groups"),
        P(("groups", "fsdp"), None, None),
        P(("groups", "fsdp"), None, None),
        P(("groups", "fsdp"), None, None),
    )
    return jax.shard_map(
        local,
        mesh=mesh,
        in_specs=placed,
        out_specs=(
            P(("groups", "fsdp"), None),
            P(("groups", "fsdp"), None),
            P(("groups", "fsdp"), None, None),
            P(("groups", "fsdp"), None, None),
            P(("groups", "fsdp"), None, None),
        ),
        check_vma=False,
    )
```

time: 464 us -> 183 us (0.39)
  waiting for transfers between devices: 358 us -> 74.1 us
  Pallas kernels: 0 us -> 51.2 us
  blocking collectives: 45.9 us -> 0 us
  starting transfers between devices: 0.16 us -> 33.1 us
  matrix products: 36.8 us -> 3.86 us
  between operations: 13.8 us -> 1.13 us
  local copies, waits for them, and re-layouts: 1.54 us -> 12.5 us
    reduce_scatter x2 -> x0, waiting for transfers between devices: 268 us -> none  [the longest x1 137 us: local(): lax.psum_scatter(down_grad, 'fsdp', scatter_dimension=0, tiled=True)]
    all_gather x2 -> x0, waiting for transfers between devices: 89.5 us -> none  [the longest x1 62.1 us: local(): weight = lax.all_gather(base_weight, 'fsdp', axis=0, tiled=True)]
    ppermute x0 -> x33, waiting for transfers between devices: none -> 74.1 us  [the longest x18 61.1 us: step(): return lax.ppermute(x, 'fsdp', [(d, d ^ flip) for d in range(self.devices)])]
    pallas_call x0 -> x24, Pallas kernels: none -> 51.2 us  [the longest x2 15.8 us: frozen(): pl.pallas_call(functools.partial(frozen_kernel, half, width, scale), grid...]
    all_gather x1 -> x0, blocking collectives: 45.9 us -> none  [local(): lax.all_gather(compute[:, feature_width:], 'fsdp', axis=0, tiled=True)]
    ppermute x0 -> x33, starting transfers between devices: none -> 33.1 us  [the longest x18 22.7 us: step(): return lax.ppermute(x, 'fsdp', [(d, d ^ flip) for d in range(self.devices)])]
    dot_general x8 -> x3, matrix products: 36.8 us -> 3.86 us  [dot(): return lax.dot_general(a, b, dims, preferred_element_type=f32)]
  transfers between devices with their start and end apart: 4 -> 33, of which waited for: 4 -> 14; matrix products, arithmetic and copies ran while one was open for 8% -> 10% of each run, Pallas kernels for 0% -> 26%
where the time goes in v3:
time: 183 us; the launch traced here: 182 us
  waiting for transfers between devices  74.1 us (40%)
  Pallas kernels  51.2 us (28%)
  starting transfers between devices  33.1 us (18%)
  local copies, waits for them, and re-layouts  12.5 us (7%)
  other arithmetic  6.06 us (3%)
  matrix products  3.86 us (2%)
    ppermute x18, waiting for transfers between devices, step(): return lax.ppermute(x, 'fsdp', [(d, d ^ flip) for d in range(self.devices)])  61.1 us
    ppermute x18, starting transfers between devices, step(): return lax.ppermute(x, 'fsdp', [(d, d ^ flip) for d in range(self.devices)])  22.7 us
    pallas_call x2, Pallas kernels, frozen(): pl.pallas_call(functools.partial(frozen_kernel, half, width, scale), grid...  15.8 us
    ppermute x15, waiting for transfers between devices, member(): return lax.ppermute(x, 'fsdp', [(i, i ^ k) for i in range(self.devices)])  13.1 us
    ppermute x15, starting transfers between devices, member(): return lax.ppermute(x, 'fsdp', [(i, i ^ k) for i in range(self.devices)])  10.4 us
    pallas_call x2, Pallas kernels, project(): pl.pallas_call(functools.partial(project_kernel, add.shape[0] // team), g...  8.86 us
    pallas_call x1, Pallas kernels, merge(): pl.pallas_call(functools.partial(merge_kernel, width, quarter), grid_spec...  6.41 us
    pallas_call x1, Pallas kernels, deal(): pl.pallas_call(functools.partial(deal_kernel, width), grid_spec=pltpu.Pre...  6.36 us
  transfers between devices with their start and end apart: 33, of which 14 were waited for; matrix products, arithmetic and copies ran while one was open for 10% of the time, Pallas kernels for 26%

profile of v3, /device:TPU:0, one launch (start us, length us, event | category | flops | bytes accessed | tf_op | source)
XLA Modules:
  0.0 182.0 jit_solution(16985974685877224127)
XLA Ops:
  1.9 1.8 shard_map.147
  4.2 2.5 %collective-permute-start.4 = (bf16[16,2560]{1,0:T(8,128)(2,1)}, bf16[16,2560]{1,0:T(8,128)(2,1)S(1)}, u32[]{:S(2)}, u32[]{:S(2)}) collective-permute-start(bf16[16,2560]{1,0:T(8,128)(2,1)} %get-tuple-element.52), channel_id=1, source_target_pairs={{0,2},{1,3},{2,0},{3,1},{4,6},{5,7},{6,4},{7,5},{8,10},{9,11},{10,... | collective-permute-start | bytes 245768 | tf_op jit(solution)/shard_map/ppermute | solution.py:51
  6.8 2.8 %collective-permute-start.8 = (bf16[256,512]{1,0:T(8,128)(2,1)}, bf16[256,512]{1,0:T(8,128)(2,1)S(1)}, u32[]{:S(2)}, u32[]{:S(2)}) collective-permute-start(bf16[256,512]{1,0:T(8,128)(2,1)} %refs_0_.1), channel_id=1, source_target_pairs={{0,16},{1,17},{2,18},{3,19},{4,20},{5,21},{6,22},{7,23},{8,24},{9,... | collective-permute-start | bytes 786440 | tf_op jit(solution)/shard_map/ppermute | solution.py:55
  12.1 1.7 shard_map.148
  13.8 1.7 collective-permute-start.7
  16.4 1.6 pad_maximum_fusion.5.t_ref
  18.0 6.4 %shard_map.146 = (bf16[192,2048]{1,0:T(8,128)(2,1)}, bf16[192,2688]{1,0:T(8,128)(2,1)}, bf16[192,2688]{1,0:T(8,128)(2,1)}, bf16[192,2688]{1,0:T(8,128)(2,1)}) custom-call(s32[9]{0:T(128)} %pad_add_fusion.info, bf16[192,8192]{1,0:T(8,128)(2,1)} %x_ref.1, bf16[192,640]{1,0:T(8,128)(2,1)} %pad_maximum_fusion.5.t_ref), custom_call_target="tpu_custom_call" | custom-call | bytes 6291456 | tf_op jit(solution)/shard_map/pallas_call | solution.py:212
  26.9 4.0 %collective-permute-done.6.refs_1_ = bf16[64,512]{1,0:T(8,128)(2,1)S(1)} collective-permute-done((bf16[64,512]{1,0:T(8,128)(2,1)S(1)}, bf16[64,512]{1,0:T(8,128)(2,1)S(1)}, u32[]{:S(2)}, u32[]{:S(2)}) %collective-permute-start.6) | collective-permute-done | bytes 65568 | tf_op jit(solution)/shard_map/ppermute | solution.py:55
  30.9 2.7 %collective-permute-start.9 = (bf16[128,512]{1,0:T(8,128)(2,1)S(1)}, bf16[128,512]{1,0:T(8,128)(2,1)S(1)}, u32[]{:S(2)}, u32[]{:S(2)}) collective-permute-start(bf16[128,512]{1,0:T(8,128)(2,1)S(1)} %get-tuple-element.56.refs_0_), channel_id=1, source_target_pairs={{0,16},{1,17},{2,18},{3,19},{4,20},{5,21},{6,22},{7,23},{8,24},{9,... | collective-permute-start | bytes 393224 | tf_op jit(solution)/shard_map/ppermute | solution.py:55
  33.6 6.4 %collective-permute-done.9.refs_1_ = bf16[128,512]{1,0:T(8,128)(2,1)S(1)} collective-permute-done((bf16[128,512]{1,0:T(8,128)(2,1)S(1)}, bf16[128,512]{1,0:T(8,128)(2,1)S(1)}, u32[]{:S(2)}, u32[]{:S(2)}) %collective-permute-start.9) | collective-permute-done | bytes 131104 | tf_op jit(solution)/shard_map/ppermute | solution.py:55
  42.6 6.6 %collective-permute-done.10.refs_1_ = bf16[256,512]{1,0:T(8,128)(2,1)S(1)} collective-permute-done((bf16[256,512]{1,0:T(8,128)(2,1)S(1)}, bf16[256,512]{1,0:T(8,128)(2,1)S(1)}, u32[]{:S(2)}, u32[]{:S(2)}) %collective-permute-start.10) | collective-permute-done | bytes 262176 | tf_op jit(solution)/shard_map/ppermute | solution.py:55
  49.3 1.9 %collective-permute-start.11 = (bf16[128,2048]{1,0:T(8,128)(2,1)S(1)}, bf16[128,2048]{1,0:T(8,128)(2,1)}, u32[]{:S(2)}, u32[]{:S(2)}) collective-permute-start(bf16[128,2048]{1,0:T(8,128)(2,1)S(1)} %get-tuple-element.59.refs_0_), channel_id=1, source_target_pairs={{0,16},{1,17},{2,18},{3,19},{4,20},{5,21},{6,22},{7,23},{8,24},{9,... | collective-permute-start | bytes 1572872 | tf_op jit(solution)/shard_map/ppermute | solution.py:55
  54.6 14.1 %collective-permute-done.12.refs_1_ = bf16[512,512]{1,0:T(8,128)(2,1)S(1)} collective-permute-done((bf16[512,512]{1,0:T(8,128)(2,1)S(1)}, bf16[512,512]{1,0:T(8,128)(2,1)S(1)}, u32[]{:S(2)}, u32[]{:S(2)}) %collective-permute-start.12) | collective-permute-done | bytes 524320 | tf_op jit(solution)/shard_map/ppermute | solution.py:55
  71.3 2.3 %collective-permute-done.11.refs_1_ = bf16[128,2048]{1,0:T(8,128)(2,1)} collective-permute-done((bf16[128,2048]{1,0:T(8,128)(2,1)S(1)}, bf16[128,2048]{1,0:T(8,128)(2,1)}, u32[]{:S(2)}, u32[]{:S(2)}) %collective-permute-start.11) | collective-permute-done | bytes 524320 | tf_op jit(solution)/shard_map/ppermute | solution.py:55
  80.9 4.4 %shard_map.156.refs_2_.refs_0_ = f32[64,192]{1,0:T(8,128)S(1)} custom-call(bf16[192,2048]{1,0:T(8,128)(2,1)} %get-tuple-element.57.refs_0_.refs_1_, bf16[192,2688]{1,0:T(8,128)(2,1)} %collective-permute-done.refs_1_.refs_2_.refs_3_, bf16[192,2688]{1,0:T(8,128)(2,1)} %collective-permute-done.1.refs_2_.refs_0_.refs_1_, ...), custom_call_target="tpu_custom_call" | custom-call | flops 805306368 | bytes 4194304 | tf_op jit(solution)/shard_map/pallas_call | solution.py:300
  87.0 5.6 %shard_map.153 = (bf16[256,1024]{1,0:T(8,128)(2,1)}, bf16[256,1024]{1,0:T(8,128)(2,1)}, bf16[256,1024]{1,0:T(8,128)(2,1)}, bf16[256,1024]{1,0:T(8,128)(2,1)}) custom-call(bf16[512,768]{1,0:T(8,128)(2,1)S(1)} %select_convert_fusion.2.low_ref, bf16[512,768]{1,0:T(8,128)(2,1)S(1)} %select_convert_fusion.1.low_two_ref, ...), custom_call_target="tpu_custom_call" | custom-call | flops 1610612736 | bytes 5242880 | tf_op jit(solution)/shard_map/pallas_call | solution.py:257
  92.6 2.6 %select_convert_fusion.refs_11_ = bf16[768,512]{1,0:T(8,128)(2,1)} fusion(bf16[768,512]{1,0:T(8,128)(2,1)} %pad_maximum_fusion.refs_10_, bf16[512,512]{1,0:T(8,128)(2,1)S(1)} %shard_map.152.refs_7_, s32[512]{0:T(512)S(1)} %add.90, s32[768]{0:T(1024)S(1)} %convert_reduce_fusion), kind=kOutput, calls=%fused_computation.1 | convolution fusion | flops 404226048 | bytes 2102272 | tf_op jit(solution)/shard_map/dot_general | solution.py:26
  95.2 2.1 %collective-permute-done.13.refs_6_.refs_7_.refs_4_.refs_3_ = bf16[256,2048]{1,0:T(8,128)(2,1)} collective-permute-done((bf16[256,2048]{1,0:T(8,128)(2,1)S(1)}, bf16[256,2048]{1,0:T(8,128)(2,1)}, u32[]{:S(2)}, u32[]{:S(2)}) %collective-permute-start.13) | collective-permute-done | bytes 1048608 | tf_op jit(solution)/shard_map/ppermute | solution.py:55
  97.3 1.7 collective-permute-start.21
  99.6 7.9 %shard_map.159 = (bf16[192,2560]{1,0:T(8,128)(2,1)}, bf16[192,2560]{1,0:T(8,128)(2,1)}, f32[192,512]{1,0:T(8,128)}) custom-call(s32[9]{0:T(128)S(1)} %copy-done.16, bf16[192,2688]{1,0:T(8,128)(2,1)} %collective-permute-done.1.refs_2_.refs_0_.refs_1_, bf16[192,2688]{1,0:T(8,128)(2,1)} %collective-permute-done.1.refs_2_.refs_0_.refs_1_, ...), custom_call_target="tpu_custom_call" | custom-call | flops 2415919104 | bytes 7340032 | tf_op jit(solution)/shard_map/pallas_call | solution.py:397
  107.5 4.4 %shard_map.161.refs_0_ = f32[64,192]{1,0:T(8,128)S(1)} custom-call(bf16[192,2048]{1,0:T(8,128)(2,1)} %get-tuple-element.57.refs_0_.refs_1_, bf16[192,2688]{1,0:T(8,128)(2,1)} %collective-permute-done.refs_1_.refs_2_.refs_3_, bf16[192,2688]{1,0:T(8,128)(2,1)} %collective-permute-done.1.refs_2_.refs_0_.refs_1_, ...), custom_call_target="tpu_custom_call" | custom-call | flops 805306368 | bytes 4194304 | tf_op jit(solution)/shard_map/pallas_call | solution.py:300
  114.8 1.7 collective-permute-done.19.refs_2_
  118.7 5.3 %collective-permute-done.23.refs_4_.refs_1_ = f32[256,128]{1,0:T(8,128)S(1)} collective-permute-done((f32[256,128]{1,0:T(8,128)S(1)}, f32[256,128]{1,0:T(8,128)S(1)}, u32[]{:S(2)}, u32[]{:S(2)}) %collective-permute-start.23) | collective-permute-done | bytes 131104 | tf_op jit(solution)/shard_map/ppermute | solution.py:55
  124.3 3.0 %collective-permute-start.24 = (bf16[128,1024]{1,0:T(8,128)(2,1)S(1)}, bf16[128,1024]{1,0:T(8,128)(2,1)S(1)}, u32[]{:S(2)}, u32[]{:S(2)}) collective-permute-start(bf16[128,1024]{1,0:T(8,128)(2,1)S(1)} %get-tuple-element.74), channel_id=1, source_target_pairs={{0,16},{1,17},{2,18},{3,19},{4,20},{5,21},{6,22},{7,23},{8,24},{9,... | collective-permute-start | bytes 786440 | tf_op jit(solution)/shard_map/ppermute | solution.py:55
  129.2 12.3 %collective-permute-done.28.refs_1_ = f32[128,128]{1,0:T(8,128)S(1)} collective-permute-done((f32[128,128]{1,0:T(8,128)S(1)}, f32[128,128]{1,0:T(8,128)S(1)}, u32[]{:S(2)}, u32[]{:S(2)}) %collective-permute-start.28) | collective-permute-done | bytes 65568 | tf_op jit(solution)/shard_map/ppermute | solution.py:55
  141.5 1.7 collective-permute-start.29
  143.8 7.9 %shard_map.158 = (bf16[192,2560]{1,0:T(8,128)(2,1)}, bf16[192,2560]{1,0:T(8,128)(2,1)}, f32[192,512]{1,0:T(8,128)}) custom-call(s32[9]{0:T(128)S(1)} %copy-done.16, bf16[192,2048]{1,0:T(8,128)(2,1)} %get-tuple-element.57.refs_0_.refs_1_, bf16[192,2048]{1,0:T(8,128)(2,1)} %get-tuple-element.57.refs_0_.refs_1_, ...), custom_call_target="tpu_custom_call" | custom-call | flops 2415919104 | bytes 7340032 | tf_op jit(solution)/shard_map/pallas_call | solution.py:397
  153.3 8.1 %collective-permute-done.27 = bf16[64,1024]{1,0:T(8,128)(2,1)S(1)} collective-permute-done((bf16[64,1024]{1,0:T(8,128)(2,1)S(1)}, bf16[64,1024]{1,0:T(8,128)(2,1)S(1)}, u32[]{:S(2)}, u32[]{:S(2)}) %collective-permute-start.27) | collective-permute-done | bytes 131104 | tf_op jit(solution)/shard_map/ppermute | solution.py:55
  161.6 1.6 collective-permute-start.31
  163.5 8.4 %collective-permute-done.17.refs_3_ = bf16[192,2560]{1,0:T(8,128)(2,1)S(1)} collective-permute-done((bf16[192,2560]{1,0:T(8,128)(2,1)S(1)}, bf16[192,2560]{1,0:T(8,128)(2,1)S(1)}, u32[]{:S(2)}, u32[]{:S(2)}) %collective-permute-start.17) | collective-permute-done | bytes 983072 | tf_op jit(solution)/shard_map/ppermute | solution.py:51
  173.3 6.4 %shard_map.163 = bf16[192,8192]{1,0:T(8,128)(2,1)} custom-call(s32[9]{0:T(128)} %pad_add_fusion.info, bf16[192,2560]{1,0:T(8,128)(2,1)} %get-tuple-element.66.refs_0_, bf16[192,2560]{1,0:T(8,128)(2,1)} %copy-done.21, bf16[192,2560]{1,0:T(8,128)(2,1)} %copy-done.19, bf16[192,2560]{1,0:T(8,128)(2,1)} %copy-done.20), custom_call_target="tpu_custom_call" | custom-call | bytes 7864320 | tf_op jit(solution)/shard_map/pallas_call | solution.py:431
  179.8 2.2 %shard_map.169 = (f32[16,8704]{1,0:T(8,128)}, f32[16,8704]{1,0:T(8,128)}, f32[16,8704]{1,0:T(8,128)}) custom-call(s32[9]{0:T(128)S(1)} %copy-done.15, f32[16,8704]{1,0:T(8,128)S(1)} %bitcast.17, f32[16,8704]{1,0:T(8,128)S(1)} %bitcast.18, f32[16,8704]{1,0:T(8,128)S(1)} %bitcast.19, f32[16,2176]{1,0:T(8,128)S(1)} %slice.69.refs_0_, ...), custom_call_target="tpu_custom_call" | custom-call | flops 2785280 | bytes 4456448 | tf_op jit(solution)/shard_map/pallas_call | solution.py:466
  (154 shorter events, 37.1 us)
Async XLA Ops:
  3.7 5.9 %collective-permute-start.3 = (bf16[16,2560]{1,0:T(8,128)(2,1)}, bf16[16,2560]{1,0:T(8,128)(2,1)S(1)}, u32[]{:S(2)}, u32[]{:S(2)}) collective-permute-start(bf16[16,2560]{1,0:T(8,128)(2,1)} %get-tuple-element.51), channel_id=1, source_target_pairs={{0,1},{1,0},{2,3},{3,2},{4,5},{5,4},{6,7},{7,6},{8,9},{9,8},{10,11... | collective-permute-start | bytes 245768 | tf_op jit(solution)/shard_map/ppermute | solution.py:51
  4.2 5.9 %collective-permute-start.4 = (bf16[16,2560]{1,0:T(8,128)(2,1)}, bf16[16,2560]{1,0:T(8,128)(2,1)S(1)}, u32[]{:S(2)}, u32[]{:S(2)}) collective-permute-start(bf16[16,2560]{1,0:T(8,128)(2,1)} %get-tuple-element.52), channel_id=1, source_target_pairs={{0,2},{1,3},{2,0},{3,1},{4,6},{5,7},{6,4},{7,5},{8,10},{9,11},{10,... | collective-permute-start | bytes 245768 | tf_op jit(solution)/shard_map/ppermute | solution.py:51
  6.7 4.8 %collective-permute-start.5 = (bf16[16,2560]{1,0:T(8,128)(2,1)}, bf16[16,2560]{1,0:T(8,128)(2,1)S(1)}, u32[]{:S(2)}, u32[]{:S(2)}) collective-permute-start(bf16[16,2560]{1,0:T(8,128)(2,1)} %get-tuple-element.53), channel_id=1, source_target_pairs={{0,3},{1,2},{2,1},{3,0},{4,7},{5,6},{6,5},{7,4},{8,11},{9,10},{10,... | collective-permute-start | bytes 245768 | tf_op jit(solution)/shard_map/ppermute | solution.py:51
  6.8 19.5 %collective-permute-start.8 = (bf16[256,512]{1,0:T(8,128)(2,1)}, bf16[256,512]{1,0:T(8,128)(2,1)S(1)}, u32[]{:S(2)}, u32[]{:S(2)}) collective-permute-start(bf16[256,512]{1,0:T(8,128)(2,1)} %refs_0_.1), channel_id=1, source_target_pairs={{0,16},{1,17},{2,18},{3,19},{4,20},{5,21},{6,22},{7,23},{8,24},{9,... | collective-permute-start | bytes 786440 | tf_op jit(solution)/shard_map/ppermute | solution.py:55
  13.8 17.0 %collective-permute-start.7 = (bf16[64,2048]{1,0:T(8,128)(2,1)}, bf16[64,2048]{1,0:T(8,128)(2,1)S(1)}, u32[]{:S(2)}, u32[]{:S(2)}) collective-permute-start(bf16[64,2048]{1,0:T(8,128)(2,1)} %get-tuple-element.55.refs_2_), channel_id=1, source_target_pairs={{0,4},{1,5},{2,6},{3,7},{4,0},{5,1},{6,2},{7,3},{8,12},{9,13},{10,... | collective-permute-start | bytes 786440 | tf_op jit(solution)/shard_map/ppermute | solution.py:55
  24.4 51.0 %collective-permute-start = (bf16[192,2688]{1,0:T(8,128)(2,1)}, bf16[192,2688]{1,0:T(8,128)(2,1)}, u32[]{:S(2)}, u32[]{:S(2)}) collective-permute-start(bf16[192,2688]{1,0:T(8,128)(2,1)} %get-tuple-element.47), channel_id=1, source_target_pairs={{0,1},{1,0},{2,3},{3,2},{4,5},{5,4},{6,7},{7,6},{8,9},{9,8},{10,11... | collective-permute-start | bytes 3096584 | tf_op jit(solution)/shard_map/ppermute | solution.py:51
  24.7 51.7 %collective-permute-start.1 = (bf16[192,2688]{1,0:T(8,128)(2,1)}, bf16[192,2688]{1,0:T(8,128)(2,1)}, u32[]{:S(2)}, u32[]{:S(2)}) collective-permute-start(bf16[192,2688]{1,0:T(8,128)(2,1)} %get-tuple-element.48), channel_id=1, source_target_pairs={{0,2},{1,3},{2,0},{3,1},{4,6},{5,7},{6,4},{7,5},{8,10},{9,11},{10,... | collective-permute-start | bytes 3096584 | tf_op jit(solution)/shard_map/ppermute | solution.py:51
  26.2 51.2 %collective-permute-start.2 = (bf16[192,2688]{1,0:T(8,128)(2,1)}, bf16[192,2688]{1,0:T(8,128)(2,1)}, u32[]{:S(2)}, u32[]{:S(2)}) collective-permute-start(bf16[192,2688]{1,0:T(8,128)(2,1)} %get-tuple-element.49), channel_id=1, source_target_pairs={{0,3},{1,2},{2,1},{3,0},{4,7},{5,6},{6,5},{7,4},{8,11},{9,10},{10,... | collective-permute-start | bytes 3096584 | tf_op jit(solution)/shard_map/ppermute | solution.py:51
  26.3 4.6 %collective-permute-start.6 = (bf16[64,512]{1,0:T(8,128)(2,1)S(1)}, bf16[64,512]{1,0:T(8,128)(2,1)S(1)}, u32[]{:S(2)}, u32[]{:S(2)}) collective-permute-start(bf16[64,512]{1,0:T(8,128)(2,1)S(1)} %copy-done.12), channel_id=1, source_target_pairs={{0,4},{1,5},{2,6},{3,7},{4,0},{5,1},{6,2},{7,3},{8,12},{9,13},{10,... | collective-permute-start | bytes 196616 | tf_op jit(solution)/shard_map/ppermute | solution.py:55
  30.9 9.0 %collective-permute-start.9 = (bf16[128,512]{1,0:T(8,128)(2,1)S(1)}, bf16[128,512]{1,0:T(8,128)(2,1)S(1)}, u32[]{:S(2)}, u32[]{:S(2)}) collective-permute-start(bf16[128,512]{1,0:T(8,128)(2,1)S(1)} %get-tuple-element.56.refs_0_), channel_id=1, source_target_pairs={{0,16},{1,17},{2,18},{3,19},{4,20},{5,21},{6,22},{7,23},{8,24},{9,... | collective-permute-start | bytes 393224 | tf_op jit(solution)/shard_map/ppermute | solution.py:55
  40.0 9.3 %collective-permute-start.10 = (bf16[256,512]{1,0:T(8,128)(2,1)S(1)}, bf16[256,512]{1,0:T(8,128)(2,1)S(1)}, u32[]{:S(2)}, u32[]{:S(2)}) collective-permute-start(bf16[256,512]{1,0:T(8,128)(2,1)S(1)} %shard_map.151.refs_0_), channel_id=1, source_target_pairs={{0,8},{1,9},{2,10},{3,11},{4,12},{5,13},{6,14},{7,15},{8,0},{9,1},... | collective-permute-start | bytes 786440 | tf_op jit(solution)/shard_map/ppermute | solution.py:55
  41.3 27.4 %collective-permute-start.12 = (bf16[512,512]{1,0:T(8,128)(2,1)S(1)}, bf16[512,512]{1,0:T(8,128)(2,1)S(1)}, u32[]{:S(2)}, u32[]{:S(2)}) collective-permute-start(bf16[512,512]{1,0:T(8,128)(2,1)S(1)} %shard_map.149.refs_4_.refs_0_), channel_id=1, source_target_pairs={{0,8},{1,9},{2,10},{3,11},{4,12},{5,13},{6,14},{7,15},{8,0},{9,1},... | collective-permute-start | bytes 1572872 | tf_op jit(solution)/shard_map/ppermute | solution.py:55
  49.3 24.4 %collective-permute-start.11 = (bf16[128,2048]{1,0:T(8,128)(2,1)S(1)}, bf16[128,2048]{1,0:T(8,128)(2,1)}, u32[]{:S(2)}, u32[]{:S(2)}) collective-permute-start(bf16[128,2048]{1,0:T(8,128)(2,1)S(1)} %get-tuple-element.59.refs_0_), channel_id=1, source_target_pairs={{0,16},{1,17},{2,18},{3,19},{4,20},{5,21},{6,22},{7,23},{8,24},{9,... | collective-permute-start | bytes 1572872 | tf_op jit(solution)/shard_map/ppermute | solution.py:55
  70.7 24.6 %collective-permute-start.14 = (bf16[1024,512]{1,0:T(8,128)(2,1)S(1)}, bf16[1024,512]{1,0:T(8,128)(2,1)}, u32[]{:S(2)}, u32[]{:S(2)}) collective-permute-start(bf16[1024,512]{1,0:T(8,128)(2,1)S(1)} %shard_map.154.refs_2_.refs_8_), channel_id=1, source_target_pairs={{0,4},{1,5},{2,6},{3,7},{4,0},{5,1},{6,2},{7,3},{8,12},{9,13},{10,... | collective-permute-start | bytes 3145736 | tf_op jit(solution)/shard_map/ppermute | solution.py:55
  74.8 22.5 %collective-permute-start.13 = (bf16[256,2048]{1,0:T(8,128)(2,1)S(1)}, bf16[256,2048]{1,0:T(8,128)(2,1)}, u32[]{:S(2)}, u32[]{:S(2)}) collective-permute-start(bf16[256,2048]{1,0:T(8,128)(2,1)S(1)} %shard_map.155.refs_4_.refs_5_), channel_id=1, source_target_pairs={{0,8},{1,9},{2,10},{3,11},{4,12},{5,13},{6,14},{7,15},{8,0},{9,1},... | collective-permute-start | bytes 3145736 | tf_op jit(solution)/shard_map/ppermute | solution.py:55
  97.3 26.7 %collective-permute-start.21 = (bf16[256,1024]{1,0:T(8,128)(2,1)}, bf16[256,1024]{1,0:T(8,128)(2,1)S(1)}, u32[]{:S(2)}, u32[]{:S(2)}) collective-permute-start(bf16[256,1024]{1,0:T(8,128)(2,1)} %get-tuple-element.69), channel_id=1, source_target_pairs={{0,8},{1,9},{2,10},{3,11},{4,12},{5,13},{6,14},{7,15},{8,0},{9,1},... | collective-permute-start | bytes 1572872 | tf_op jit(solution)/shard_map/ppermute | solution.py:55
  99.0 24.9 %collective-permute-start.22 = (bf16[256,1024]{1,0:T(8,128)(2,1)}, bf16[256,1024]{1,0:T(8,128)(2,1)S(1)}, u32[]{:S(2)}, u32[]{:S(2)}) collective-permute-start(bf16[256,1024]{1,0:T(8,128)(2,1)} %get-tuple-element.71), channel_id=1, source_target_pairs={{0,4},{1,5},{2,6},{3,7},{4,0},{5,1},{6,2},{7,3},{8,12},{9,13},{10,... | collective-permute-start | bytes 1572872 | tf_op jit(solution)/shard_map/ppermute | solution.py:55
  112.0 4.5 %collective-permute-start.19 = (f32[64,192]{1,0:T(8,128)S(1)}, f32[64,192]{1,0:T(8,128)S(1)}, u32[]{:S(2)}, u32[]{:S(2)}) collective-permute-start(f32[64,192]{1,0:T(8,128)S(1)} %shard_map.161.refs_0_), channel_id=1, source_target_pairs={{0,2},{1,3},{2,0},{3,1},{4,6},{5,7},{6,4},{7,5},{8,10},{9,11},{10,... | collective-permute-start | bytes 147464 | tf_op jit(solution)/shard_map/ppermute | solution.py:51
  113.6 4.0 %collective-permute-start.20 = (f32[64,192]{1,0:T(8,128)S(1)}, f32[64,192]{1,0:T(8,128)S(1)}, u32[]{:S(2)}, u32[]{:S(2)}) collective-permute-start(f32[64,192]{1,0:T(8,128)S(1)} %shard_map.161.refs_0_), channel_id=1, source_target_pairs={{0,3},{1,2},{2,1},{3,0},{4,7},{5,6},{6,5},{7,4},{8,11},{9,10},{10,... | collective-permute-start | bytes 147464 | tf_op jit(solution)/shard_map/ppermute | solution.py:51
  118.3 5.6 %collective-permute-start.23 = (f32[256,128]{1,0:T(8,128)S(1)}, f32[256,128]{1,0:T(8,128)S(1)}, u32[]{:S(2)}, u32[]{:S(2)}) collective-permute-start(f32[256,128]{1,0:T(8,128)S(1)} %get-tuple-element.72), channel_id=1, source_target_pairs={{0,8},{1,9},{2,10},{3,11},{4,12},{5,13},{6,14},{7,15},{8,0},{9,1},... | collective-permute-start | bytes 393224 | tf_op jit(solution)/shard_map/ppermute | solution.py:55
  124.3 18.9 %collective-permute-start.24 = (bf16[128,1024]{1,0:T(8,128)(2,1)S(1)}, bf16[128,1024]{1,0:T(8,128)(2,1)S(1)}, u32[]{:S(2)}, u32[]{:S(2)}) collective-permute-start(bf16[128,1024]{1,0:T(8,128)(2,1)S(1)} %get-tuple-element.74), channel_id=1, source_target_pairs={{0,16},{1,17},{2,18},{3,19},{4,20},{5,21},{6,22},{7,23},{8,24},{9,... | collective-permute-start | bytes 786440 | tf_op jit(solution)/shard_map/ppermute | solution.py:55
  127.3 15.9 %collective-permute-start.25 = (bf16[128,1024]{1,0:T(8,128)(2,1)S(1)}, bf16[128,1024]{1,0:T(8,128)(2,1)S(1)}, u32[]{:S(2)}, u32[]{:S(2)}) collective-permute-start(bf16[128,1024]{1,0:T(8,128)(2,1)S(1)} %get-tuple-element.76), channel_id=1, source_target_pairs={{0,8},{1,9},{2,10},{3,11},{4,12},{5,13},{6,14},{7,15},{8,0},{9,1},... | collective-permute-start | bytes 786440 | tf_op jit(solution)/shard_map/ppermute | solution.py:55
  127.6 13.9 %collective-permute-start.28 = (f32[128,128]{1,0:T(8,128)S(1)}, f32[128,128]{1,0:T(8,128)S(1)}, u32[]{:S(2)}, u32[]{:S(2)}) collective-permute-start(f32[128,128]{1,0:T(8,128)S(1)} %get-tuple-element.83), channel_id=1, source_target_pairs={{0,16},{1,17},{2,18},{3,19},{4,20},{5,21},{6,22},{7,23},{8,24},{9,... | collective-permute-start | bytes 196616 | tf_op jit(solution)/shard_map/ppermute | solution.py:55
  127.7 35.5 %collective-permute-start.16 = (bf16[192,2560]{1,0:T(8,128)(2,1)S(1)}, bf16[192,2560]{1,0:T(8,128)(2,1)S(1)}, u32[]{:S(2)}, u32[]{:S(2)}) collective-permute-start(bf16[192,2560]{1,0:T(8,128)(2,1)S(1)} %copy-done.29), channel_id=1, source_target_pairs={{0,2},{1,3},{2,0},{3,1},{4,6},{5,7},{6,4},{7,5},{8,10},{9,11},{10,... | collective-permute-start | bytes 2949128 | tf_op jit(solution)/shard_map/ppermute | solution.py:51
  129.2 42.8 %collective-permute-start.17 = (bf16[192,2560]{1,0:T(8,128)(2,1)S(1)}, bf16[192,2560]{1,0:T(8,128)(2,1)S(1)}, u32[]{:S(2)}, u32[]{:S(2)}) collective-permute-start(bf16[192,2560]{1,0:T(8,128)(2,1)S(1)} %copy-done.28), channel_id=1, source_target_pairs={{0,3},{1,2},{2,1},{3,0},{4,7},{5,6},{6,5},{7,4},{8,11},{9,10},{10,... | collective-permute-start | bytes 2949128 | tf_op jit(solution)/shard_map/ppermute | solution.py:51
  141.5 10.2 %collective-permute-start.29 = (f32[64,128]{1,0:T(8,128)S(1)}, f32[64,128]{1,0:T(8,128)S(1)}, u32[]{:S(2)}, u32[]{:S(2)}) collective-permute-start(f32[64,128]{1,0:T(8,128)S(1)} %get-tuple-element.85), channel_id=1, source_target_pairs={{0,4},{1,5},{2,6},{3,7},{4,0},{5,1},{6,2},{7,3},{8,12},{9,13},{10,... | collective-permute-start | bytes 98312 | tf_op jit(solution)/shard_map/ppermute | solution.py:55
  143.3 9.9 %collective-permute-start.26 = (bf16[64,1024]{1,0:T(8,128)(2,1)S(1)}, bf16[64,1024]{1,0:T(8,128)(2,1)S(1)}, u32[]{:S(2)}, u32[]{:S(2)}) collective-permute-start(bf16[64,1024]{1,0:T(8,128)(2,1)S(1)} %get-tuple-element.78), channel_id=1, source_target_pairs={{0,4},{1,5},{2,6},{3,7},{4,0},{5,1},{6,2},{7,3},{8,12},{9,13},{10,... | collective-permute-start | bytes 393224 | tf_op jit(solution)/shard_map/ppermute | solution.py:55
  151.7 20.3 %collective-permute-start.15 = (bf16[192,2560]{1,0:T(8,128)(2,1)}, bf16[192,2560]{1,0:T(8,128)(2,1)S(1)}, u32[]{:S(2)}, u32[]{:S(2)}) collective-permute-start(bf16[192,2560]{1,0:T(8,128)(2,1)} %get-tuple-element.61), channel_id=1, source_target_pairs={{0,1},{1,0},{2,3},{3,2},{4,5},{5,4},{6,7},{7,6},{8,9},{9,8},{10,11... | collective-permute-start | bytes 2949128 | tf_op jit(solution)/shard_map/ppermute | solution.py:51
  151.8 9.6 %collective-permute-start.27 = (bf16[64,1024]{1,0:T(8,128)(2,1)S(1)}, bf16[64,1024]{1,0:T(8,128)(2,1)S(1)}, u32[]{:S(2)}, u32[]{:S(2)}) collective-permute-start(bf16[64,1024]{1,0:T(8,128)(2,1)S(1)} %get-tuple-element.80), channel_id=1, source_target_pairs={{0,16},{1,17},{2,18},{3,19},{4,20},{5,21},{6,22},{7,23},{8,24},{9,... | collective-permute-start | bytes 393224 | tf_op jit(solution)/shard_map/ppermute | solution.py:55
  161.5 18.3 %collective-permute-start.30 = (bf16[16,2176]{1,0:T(8,128)(2,1)S(1)}, bf16[16,2176]{1,0:T(8,128)(2,1)S(1)}, u32[]{:S(2)}, u32[]{:S(2)}) collective-permute-start(bf16[16,2176]{1,0:T(8,128)(2,1)S(1)} %get-tuple-element.91), channel_id=1, source_target_pairs={{0,1},{1,0},{2,3},{3,2},{4,5},{5,4},{6,7},{7,6},{8,9},{9,8},{10,11... | collective-permute-start | bytes 208904 | tf_op jit(solution)/shard_map/ppermute | solution.py:51
  161.6 18.1 %collective-permute-start.31 = (bf16[16,2176]{1,0:T(8,128)(2,1)S(1)}, bf16[16,2176]{1,0:T(8,128)(2,1)S(1)}, u32[]{:S(2)}, u32[]{:S(2)}) collective-permute-start(bf16[16,2176]{1,0:T(8,128)(2,1)S(1)} %get-tuple-element.90), channel_id=1, source_target_pairs={{0,2},{1,3},{2,0},{3,1},{4,6},{5,7},{6,4},{7,5},{8,10},{9,11},{10,... | collective-permute-start | bytes 208904 | tf_op jit(solution)/shard_map/ppermute | solution.py:51
  163.3 16.5 %collective-permute-start.32 = (bf16[16,2176]{1,0:T(8,128)(2,1)S(1)}, bf16[16,2176]{1,0:T(8,128)(2,1)S(1)}, u32[]{:S(2)}, u32[]{:S(2)}) collective-permute-start(bf16[16,2176]{1,0:T(8,128)(2,1)S(1)} %get-tuple-element.89), channel_id=1, source_target_pairs={{0,3},{1,2},{2,1},{3,0},{4,7},{5,6},{6,5},{7,4},{8,11},{9,10},{10,... | collective-permute-start | bytes 208904 | tf_op jit(solution)/shard_map/ppermute | solution.py:51
  (31 other events, 217.2 us)
